TPU v7x, 256 devices: a whole 4x4x8 slice. The times are simulated.
256 devices in a mesh: row: 16 (over y, x_hi, core), col: 16 (over x_lo, z).
Axes of the slice: x: 4 (x_hi: 2, x_lo: 2; x = x_hi * 2 + x_lo), y: 4, z: 8, core: 2. Of those that a mesh axis runs over, the one named last changes fastest.
Arguments:
- tokens: bfloat16 [1280, 10240], P('col', 'row'), may hold values from -6 to 6
- up_weight: bfloat16 [10240, 20480], P('row', 'col'), may hold values from -0.0625 to 0.0625
- down_weight: bfloat16 [20480, 10240], P('col', 'row'), may hold values from -0.0390625 to 0.0390625
- grad_out: bfloat16 [1280, 10240], P('col', 'row'), may hold values from -6 to 6
Outputs:
- mixed: bfloat16 [1280, 10240], P('col', 'row')
- input_grad: bfloat16 [1280, 10240], P('col', 'row')
- up_grad: bfloat16 [10240, 20480], P('row', 'col')
- down_grad: bfloat16 [20480, 10240], P('col', 'row')
All inputs are finite; a program needn't handle non-finite values.
Results may differ from a plain program's by a relative error of at most 0.005.
Values may be sent and summed in bfloat16 or wider, within the bound.
A program may use at most 128 MiB of HBM per device.

v0:
```python
import jax
import jax.numpy as jnp
from jax import lax
from jax.sharding import PartitionSpec as P


def gelu_back(hidden, upstream):
    _, pullback = jax.vjp(jax.nn.gelu, hidden)
    return pullback(upstream)[0].astype(jnp.bfloat16)


def contract_rows(left, right):
    return lax.dot_general(
        left, right, (((0,), (0,)), ((), ())), preferred_element_type=jnp.float32
    )


def times_trans(left, right):
    return lax.dot_general(
        left, right, (((1,), (1,)), ((), ())), preferred_element_type=jnp.float32
    )


def local(tokens, up_weight, down_weight, grad_out):
    gathered = lax.all_gather(tokens, "col", axis=0, tiled=True)
    hidden = lax.psum_scatter(
        jnp.dot(gathered, up_weight, preferred_element_type=jnp.float32),
        "row",
        scatter_dimension=1,
        tiled=True,
    )
    active = jax.nn.gelu(hidden).astype(jnp.bfloat16)
    activations = lax.all_gather(active, "row", axis=1, tiled=True)
    mixed = lax.psum_scatter(
        jnp.dot(activations, down_weight, preferred_element_type=jnp.float32),
        "col",
        scatter_dimension=0,
        tiled=True,
    ).astype(jnp.bfloat16)
    cotangent = lax.all_gather(grad_out, "col", axis=0, tiled=True)
    down_grad = contract_rows(activations, cotangent).astype(jnp.bfloat16)
    act_grad = lax.psum_scatter(
        times_trans(cotangent, down_weight), "row", scatter_dimension=1, tiled=True
    )
    hidden_grad = gelu_back(hidden, act_grad)
    grad_units = lax.all_gather(hidden_grad, "row", axis=1, tiled=True)
    up_grad = contract_rows(gathered, grad_units).astype(jnp.bfloat16)
    input_grad = lax.psum_scatter(
        times_trans(grad_units, up_weight), "col", scatter_dimension=0, tiled=True
    ).astype(jnp.bfloat16)
    return (mixed, input_grad, up_grad, down_grad)


def solution(mesh):
    placed = (P("col", "row"), P("row", "col"), P("col", "row"), P("col", "row"))
    return jax.shard_map(
        local,
        mesh=mesh,
        in_specs=placed,
        out_specs=(P("col", "row"), P("col", "row"), P("row", "col"), P("col", "row")),
        check_vma=False,
    )
```

profile of v0, /device:TPU:8, one launch (start us, length us, event | category | flops | bytes accessed | tf_op | source)
XLA Modules:
  0.0 636.6 jit_solution(14353200427918285470)
XLA Ops:
  7.2 0.7 all-gather.9.cloned.1.call-update
  8.0 0.7 all-gather.5.cloned.1.call-update
  8.7 74.5 %all-gather.9.cloned.1.call-done = bf16[1280,640]{1,0:T(8,128)(2,1)} async-done(((bf16[80,640]{1,0:T(8,128)(2,1)}), bf16[1280,640]{1,0:T(8,128)(2,1)}) %all-gather.9.cloned.1.call-update) | async-done | bytes 1638416 | tf_op jit(solution)/shard_map/all_gather | solution.py:40
  83.2 7.4 %fusion.10 = f32[1280,1280]{0,1:T(8,128)} fusion(bf16[1280,640]{1,0:T(8,128)(2,1)} %all-gather.9.cloned.1.call-done, bf16[1280,640]{1,0:T(8,128)(2,1)} %param.6), kind=kOutput, calls=%fused_computation.15 | convolution fusion | flops 2097152000 | bytes 9830400 | tf_op jit(solution)/shard_map/dot_general | solution.py:19
  90.6 0.0 reduce-scatter.5.cloned.1.call-start
  90.7 62.0 %all-gather.5.cloned.1.call-done = bf16[1280,640]{1,0:T(8,128)(2,1)} async-done(((bf16[80,640]{1,0:T(8,128)(2,1)}), bf16[1280,640]{1,0:T(8,128)(2,1)}) %all-gather.5.cloned.1.call-update) | async-done | bytes 1638416 | tf_op jit(solution)/shard_map/all_gather | solution.py:25
  152.7 6.2 fusion.8
  158.9 0.0 all-gather.11.cloned.1.call-start
  159.0 93.6 %reduce-scatter.9.cloned.1.call-done = f32[1280,80]{0,1:T(8,128)} async-done(((f32[1280,1280]{0,1:T(8,128)}), f32[1280,80]{0,1:T(8,128)}) %reduce-scatter.9.cloned.1.call-update) | async-done | bytes 409616 | tf_op jit(solution)/shard_map/reduce_scatter | solution.py:42
  252.6 102.5 %reduce-scatter.5.cloned.1.call-done = f32[1280,80]{0,1:T(8,128)} async-done(((f32[1280,1280]{0,1:T(8,128)}), f32[1280,80]{0,1:T(8,128)}) %reduce-scatter.5.cloned.1.call-update) | async-done | bytes 409616 | tf_op jit(solution)/shard_map/reduce_scatter | solution.py:26
  355.1 2.2 fusion.7
  357.3 0.5 all-gather.7.cloned.1.call-update
  357.9 55.4 %all-gather.11.cloned.1.call-done = bf16[1280,1280]{0,1:T(8,128)(2,1)} async-done(((bf16[1280,80]{0,1:T(8,128)(2,1)}), bf16[1280,1280]{0,1:T(8,128)(2,1)}) %all-gather.11.cloned.1.call-update) | async-done | bytes 3276816 | tf_op jit(solution)/shard_map/all_gather | solution.py:46
  413.3 6.4 %fusion.11 = f32[1280,640]{1,0:T(8,128)} fusion(bf16[1280,1280]{0,1:T(8,128)(2,1)} %all-gather.11.cloned.1.call-done, bf16[640,1280]{1,0:T(8,128)(2,1)S(1)} %copy-done), kind=kOutput, calls=%fused_computation.16 | convolution fusion | flops 2097152000 | bytes 8192000 | tf_op jit(solution)/shard_map/dot_general | solution.py:19
  419.7 0.2 reduce-scatter.7.cloned.1.call-start
  420.0 51.5 %all-gather.7.cloned.1.call-done = bf16[1280,1280]{0,1:T(8,128)(2,1)} async-done(((bf16[1280,80]{0,1:T(8,128)(2,1)}), bf16[1280,1280]{0,1:T(8,128)(2,1)}) %all-gather.7.cloned.1.call-update) | async-done | bytes 3276816 | tf_op jit(solution)/shard_map/all_gather | solution.py:33
  471.5 6.4 %fusion.9 = f32[1280,640]{1,0:T(8,128)} fusion(bf16[1280,1280]{0,1:T(8,128)(2,1)} %all-gather.7.cloned.1.call-done, bf16[1280,640]{1,0:T(8,128)(2,1)S(1)} %copy-done.1), kind=kOutput, calls=%fused_computation.14 | convolution fusion | flops 2097152000 | bytes 8192000 | tf_op jit(solution)/shard_map/dot_general | solution.py:35
  478.0 5.1 fusion
  483.1 2.2 copy.8
  485.3 6.3 convolution_convert_fusion
  491.6 59.9 %reduce-scatter.11.cloned.1.call-done = f32[80,640]{1,0:T(8,128)} async-done(((f32[1280,640]{1,0:T(8,128)}), f32[80,640]{1,0:T(8,128)}) %reduce-scatter.11.cloned.1.call-update) | async-done | bytes 204816 | tf_op jit(solution)/shard_map/reduce_scatter | solution.py:48
  551.5 1.6 convert_element_type.24
  553.1 75.1 %reduce-scatter.7.cloned.1.call-done = f32[80,640]{1,0:T(8,128)} async-done(((f32[1280,640]{1,0:T(8,128)}), f32[80,640]{1,0:T(8,128)}) %reduce-scatter.7.cloned.1.call-update) | async-done | bytes 204816 | tf_op jit(solution)/shard_map/reduce_scatter | solution.py:34
  628.1 1.6 convert_element_type.22
  (14 shorter events, 0.3 us)
Async XLA Ops:
  7.2 145.6 %copy-start = (bf16[640,1280]{1,0:T(8,128)(2,1)S(1)}, bf16[640,1280]{1,0:T(8,128)(2,1)}, u32[]{:S(2)}) copy-start(bf16[640,1280]{1,0:T(8,128)(2,1)} %param.5) | copy-start | bytes 4915204
  7.2 76.0 %all-gather.9.cloned.1.call-start = ((), (), s32[]{:S(2)}) async-start(), calls=%async_computation.8 | async-start | bytes 1740800 | tf_op jit(solution)/shard_map/all_gather | solution.py:40
  7.9 144.8 %all-gather.5.cloned.1.call-start = ((), (), s32[]{:S(2)}) async-start(), calls=%async_computation.4 | async-start | bytes 1740800 | tf_op jit(solution)/shard_map/all_gather | solution.py:25
  8.7 243.9 %reduce-scatter.9.cloned.1.call-start = ((), (), s32[]{:S(2)}) async-start(), calls=%async_computation.9 | async-start | bytes 6963200 | tf_op jit(solution)/shard_map/reduce_scatter | solution.py:42
  90.6 264.4 %reduce-scatter.5.cloned.1.call-start = ((), (), s32[]{:S(2)}) async-start(), calls=%async_computation.5 | async-start | bytes 6963200 | tf_op jit(solution)/shard_map/reduce_scatter | solution.py:26
  158.9 254.3 %all-gather.11.cloned.1.call-start = ((), (), s32[]{:S(2)}) async-start(), calls=%async_computation.10 | async-start | bytes 3481600 | tf_op jit(solution)/shard_map/all_gather | solution.py:46
  357.3 114.3 %all-gather.7.cloned.1.call-start = ((), (), s32[]{:S(2)}) async-start(), calls=%async_computation.6 | async-start | bytes 3481600 | tf_op jit(solution)/shard_map/all_gather | solution.py:33
  357.8 193.7 %reduce-scatter.11.cloned.1.call-start = ((), (), s32[]{:S(2)}) async-start(), calls=%async_computation.11 | async-start | bytes 3481600 | tf_op jit(solution)/shard_map/reduce_scatter | solution.py:48
  419.7 51.8 %copy-start.1 = (bf16[1280,640]{1,0:T(8,128)(2,1)S(1)}, bf16[1280,640]{1,0:T(8,128)(2,1)}, u32[]{:S(2)}) copy-start(bf16[1280,640]{1,0:T(8,128)(2,1)} %param.6) | copy-start | bytes 4915204
  419.7 208.4 %reduce-scatter.7.cloned.1.call-start = ((), (), s32[]{:S(2)}) async-start(), calls=%async_computation.7 | async-start | bytes 3481600 | tf_op jit(solution)/shard_map/reduce_scatter | solution.py:34
Sparse Core Ops, SparseCore 0:
  9.8 73.3 all-gather.8
  85.0 67.6 all-gather.4
  157.2 95.3 reduce-scatter.8
  257.6 97.3 reduce-scatter.4
  358.2 54.9 all-gather.10
  416.5 55.0 all-gather.6
  474.1 77.3 reduce-scatter.10
  554.1 74.0 reduce-scatter.6
where the time goes:
time: 637 us
  waiting for transfers between devices  577 us (91%)
  matrix products  37.9 us (6%)
  between operations  14.2 us (2%)
    reduce_scatter x1, waiting for transfers between devices, local(): lax.psum_scatter(jnp.dot(gathered, up_weight, preferred_element_type=jnp....  102 us
    reduce_scatter x1, waiting for transfers between devices, local(): lax.psum_scatter(times_trans(cotangent, down_weight), 'row', scatter_dime...  93.6 us
    reduce_scatter x1, waiting for transfers between devices, local(): lax.psum_scatter(jnp.dot(activations, down_weight, preferred_element_type...  75.1 us
    all_gather x1, waiting for transfers between devices, local(): cotangent = lax.all_gather(grad_out, 'col', axis=0, tiled=True)  74.5 us
    all_gather x1, waiting for transfers between devices, local(): gathered = lax.all_gather(tokens, 'col', axis=0, tiled=True)  62 us
    reduce_scatter x1, waiting for transfers between devices, local(): lax.psum_scatter(times_trans(grad_units, up_weight), 'col', scatter_dimen...  59.9 us
    all_gather x1, waiting for transfers between devices, local(): grad_units = lax.all_gather(hidden_grad, 'row', axis=1, tiled=True)  55.4 us
    all_gather x1, waiting for transfers between devices, local(): activations = lax.all_gather(active, 'row', axis=1, tiled=True)  51.5 us
  transfers between devices with their start and end apart: 8, of which 8 were waited for; matrix products, arithmetic and copies ran while one was open for 7% of the time, Pallas kernels for 0%

commit v1 on v0

v1 whole, which is shorter than its diff:
```python
import jax
import jax.numpy as jnp
from jax import lax
from jax.experimental import pallas as pl
from jax.experimental.pallas import tpu as pltpu
from jax.sharding import PartitionSpec as P

MESH = pl.DeviceIdType.MESH
BF = jnp.bfloat16
F32 = jnp.float32

TOK = 80
HALF = 640
WIDE = 1280
ROWS = 8 * TOK

PLACE = {0: 0, 1: 1, -1: 2, 2: 3, -2: 4, 3: 5, -3: 6, 4: 7}

C0 = 0.7978845608028654
C1 = 0.044715


def gelu(v):
    return 0.5 * v * (1.0 + jnp.tanh(C0 * (v + C1 * v * v * v)))


def gelu_slope(v):
    t = jnp.tanh(C0 * (v + C1 * v * v * v))
    return 0.5 * (1.0 + t) + 0.5 * v * (1.0 - t * t) * (C0 * (1.0 + 3.0 * C1 * v * v))


def rows_of(place):
    if isinstance(place, int):
        return pl.ds(place * TOK, TOK)
    return pl.ds(pl.multiple_of(place * TOK, TOK), TOK)


def cols_of(half):
    if isinstance(half, int):
        return pl.ds(half * HALF, HALF)
    return pl.ds(pl.multiple_of(half * HALF, HALF), HALF)


def kernel(
    tok_in, up_in, down_in, grad_in,
    mixed_out, igrad_out, upg_out, downg_out,
    up, down, tok, grad, act, hgrad, tok_o, grad_o,
    part, hid, p_send, p_recv, p_out, p_in, z_send, z_recv, f_send, f_recv,
    upg, downg, small,
    ssem, rsem, lsem,
):
    r, c = lax.axis_index("row"), lax.axis_index("col")
    y, xh, k = r // 4, (r // 2) % 2, r % 2
    xl, z = c // 8, c % 8

    def row_id(yy, hh, kk):
        return (yy * 2 + hh) * 2 + kk

    mate = (row_id(y, xh, 1 - k), c)
    yp = (row_id((y + 1) % 4, xh, k), c)
    ym = (row_id((y + 3) % 4, xh, k), c)
    across = (row_id(y, 1 - xh, k), c)
    zp = (r, xl * 8 + (z + 1) % 8)
    zm = (r, xl * 8 + (z + 7) % 8)
    other_c = (1 - xl) * 8 + z
    other0 = (row_id(y, xh, 0), other_c)
    other1 = (row_id(y, xh, 1), other_c)

    sends = []
    count = [0]

    def sem():
        count[0] += 1
        return count[0] - 1

    def rcopy(src, dst, dev):
        i = sem()
        cp = pltpu.make_async_remote_copy(
            src_ref=src, dst_ref=dst, send_sem=ssem.at[i], recv_sem=rsem.at[i],
            device_id=dev, device_id_type=MESH,
        )
        cp.start()
        sends.append(cp)
        return cp

    lcount = [0]

    def lcopy(src, dst):
        cp = pltpu.make_async_copy(src, dst, lsem.at[lcount[0]])
        lcount[0] += 1
        cp.start()
        return cp

    own_up = lcopy(up_in, up.at[pl.ds(pl.multiple_of(k * HALF, HALF), HALF)])
    own_down = lcopy(down_in, down.at[:, cols_of(k)])

    barrier = pltpu.get_barrier_semaphore()
    for dev in (mate, yp, ym, across, zp, zm, other0, other1):
        pl.semaphore_signal(barrier, inc=1, device_id=dev, device_id_type=MESH)
    pl.semaphore_wait(barrier, 8)

    def spread(src, buf):
        i, j = sem(), sem()
        dst = buf.at[rows_of(0), cols_of(k)]
        far = pltpu.make_async_remote_copy(
            src_ref=src, dst_ref=dst, send_sem=ssem.at[i], recv_sem=rsem.at[i + k],
            device_id=(row_id(y, xh, xl), other_c), device_id_type=MESH,
        )
        near = pltpu.make_async_remote_copy(
            src_ref=src, dst_ref=dst, send_sem=ssem.at[j], recv_sem=rsem.at[i + k],
            device_id=mate, device_id_type=MESH,
        )
        stay = pltpu.make_async_copy(src, dst, rsem.at[i + k])
        far.start()

        @pl.when(k != xl)
        def _():
            near.start()

        @pl.when(k == xl)
        def _():
            stay.start()

        def arrived(h):
            pltpu.make_async_copy(src, buf.at[rows_of(0), cols_of(h)], rsem.at[i + h]).wait()

        def sent():
            far.wait_send()

            @pl.when(k != xl)
            def _():
                near.wait_send()

        return arrived, sent

    tok_arrived, tok_sent = spread(tok_in, tok)
    w1 = rcopy(up_in, up.at[pl.ds(pl.multiple_of(k * HALF, HALF), HALF)], mate)
    w2 = rcopy(down_in, down.at[:, cols_of(k)], mate)
    grad_arrived, grad_sent = spread(grad_in, grad)

    class Gather:
        def __init__(self, buf, arrived):
            self.buf, self.arrived, self.got = buf, arrived, {}

        def piece(self, off, h):
            return self.buf.at[rows_of(PLACE[off]), cols_of(h)]

        def send(self, off, h, sign):
            to = off - sign
            if to == -4:
                to = 4
            cp = rcopy(self.piece(off, h), self.piece(to, h), zp if sign > 0 else zm)
            self.got[(to, h)] = cp

        def wait(self, off, h):
            cp = self.got.pop((off, h), None)
            if cp is not None:
                cp.wait_recv()

        def step(self, n):
            if n == 1:
                for h in (0, 1):
                    self.arrived(h)
                    self.send(0, h, 1)
                    self.send(0, h, -1)
            elif n < 4:
                for h in (0, 1):
                    self.wait(-(n - 1), h)
                    self.send(-(n - 1), h, 1)
                    self.wait(n - 1, h)
                    self.send(n - 1, h, -1)
            else:
                self.wait(-3, 0)
                self.send(-3, 0, 1)
                self.wait(3, 1)
                self.send(3, 1, -1)
                self.wait(-3, 1)
                self.wait(3, 0)

        def finish(self):
            self.wait(4, 0)
            self.wait(4, 1)

    def matmul(lhs, rhs, out, place, trans):
        rows = rows_of(place)

        def body(n, _):
            cols = pl.ds(pl.multiple_of(n * 256, 256), 256)
            if trans:
                v = lax.dot_general(lhs[rows, :], rhs[cols, :], (((1,), (1,)), ((), ())),
                                    preferred_element_type=F32)
            else:
                v = jnp.dot(lhs[rows, :], rhs[:, cols], preferred_element_type=F32)
            out[rows, cols] = v
            return 0

        lax.fori_loop(0, WIDE // 256, body, 0)

    class Reduce:
        def __init__(self, src, n):
            self.src, self.n, self.cp = src, n, {}

        def at(self, b, i):
            return rows_of((self.n * 2 + b) * 3 + i)

        def step1(self, b):
            s = rows_of(b * 4 + (y + 2) % 4)
            p_send[self.at(b, 0), :] = self.src[s, :].astype(BF)
            self.cp[(b, 1)] = [
                rcopy(p_send.at[self.at(b, 0), cols_of(0)], p_recv.at[self.at(b, 0), cols_of(0)], yp),
                rcopy(p_send.at[self.at(b, 0), cols_of(1)], p_recv.at[self.at(b, 0), cols_of(1)], ym),
            ]

        def step2(self, b):
            lo, hi = cols_of(0), cols_of(1)
            plus, minus = rows_of(b * 4 + (y + 1) % 4), rows_of(b * 4 + (y + 3) % 4)
            p_send[self.at(b, 1), hi] = self.src[plus, hi].astype(BF)
            p_send[self.at(b, 2), lo] = self.src[minus, lo].astype(BF)
            self.cp[(b, 1)][0].wait_recv()
            p_send[self.at(b, 1), lo] = (
                self.src[plus, lo] + p_recv[self.at(b, 0), lo].astype(F32)).astype(BF)
            first = rcopy(p_send.at[self.at(b, 1)], p_recv.at[self.at(b, 1)], yp)
            self.cp[(b, 1)][1].wait_recv()
            p_send[self.at(b, 2), hi] = (
                self.src[minus, hi] + p_recv[self.at(b, 0), hi].astype(F32)).astype(BF)
            second = rcopy(p_send.at[self.at(b, 2)], p_recv.at[self.at(b, 2)], ym)
            self.cp[(b, 2)] = [first, second]

        def total(self, b):
            for cp in self.cp[(b, 2)]:
                cp.wait_recv()
            return (self.src[rows_of(b * 4 + y), :] + p_recv[self.at(b, 1), :].astype(F32)
                    + p_recv[self.at(b, 2), :].astype(F32))

        def cross(self, b):
            t = self.total(b)

            @pl.when(xh == b)
            def _():
                hid[rows_of(self.n), :] = t

            @pl.when(xh != b)
            def _():
                p_out[rows_of(self.n), :] = t

        def send(self):
            self.x = rcopy(p_out.at[rows_of(self.n)], p_in.at[rows_of(self.n)], across)

        def result(self):
            self.x.wait_recv()
            return hid[rows_of(self.n), :] + p_in[rows_of(self.n), :]

    class Spread:
        def __init__(self, buf):
            self.buf = buf

        def piece(self, yy, hh, cols=None):
            rows = rows_of(hh * 4 + yy)
            return self.buf.at[rows] if cols is None else self.buf.at[rows, cols]

        def start(self):
            mine = self.piece(y, xh)
            self.x = rcopy(mine, mine, across)
            self.own = [rcopy(mine, mine, yp), rcopy(mine, mine, ym)]

        def second(self):
            self.x.wait_recv()
            other = self.piece(y, 1 - xh)
            self.oth = [rcopy(other, other, yp), rcopy(other, other, ym)]

        def forward(self, which):
            cps, hh = (self.own, xh) if which == 0 else (self.oth, 1 - xh)
            cps[0].wait_recv()
            p = self.piece((y + 3) % 4, hh, cols_of(0))
            f0 = rcopy(p, p, yp)
            cps[1].wait_recv()
            p = self.piece((y + 1) % 4, hh, cols_of(1))
            f1 = rcopy(p, p, ym)
            return [f0, f1]

    class ZReduce:
        def __init__(self, src, n):
            self.src, self.n = src, n

        def slot(self, off):
            return rows_of(self.n * 7 + (off + 3 if off < 4 else 0))

        def at(self, off):
            return rows_of(self.n * 8 + PLACE[off])

        def step1(self):
            lo, hi = cols_of(0), cols_of(1)
            z_send[self.at(4), :] = self.src[rows_of(PLACE[4]), :].astype(BF)
            self.plus = rcopy(z_send.at[self.at(4), lo], z_recv.at[self.at(3), lo], zp)
            self.minus = rcopy(z_send.at[self.at(4), hi], z_recv.at[self.at(-3), hi], zm)

        def step(self, off):
            lo, hi = cols_of(0), cols_of(1)
            for sign in (1, -1):
                o = off * sign
                s = rows_of(PLACE[o])
                if off == 3:
                    raw, add = (hi, lo) if sign > 0 else (lo, hi)
                    z_send[self.at(o), raw] = self.src[s, raw].astype(BF)
                    (self.plus if sign > 0 else self.minus).wait_recv()
                    z_send[self.at(o), add] = (
                        self.src[s, add] + z_recv[self.at(o), add].astype(F32)).astype(BF)
                else:
                    (self.plus if sign > 0 else self.minus).wait_recv()
                    z_send[self.at(o), :] = (
                        self.src[s, :] + z_recv[self.at(o), :].astype(F32)).astype(BF)
                to = 0 if off == 1 else o - sign
                dst = z_recv.at[self.at(to if off > 1 else (0 if sign > 0 else 4))]
                cp = rcopy(z_send.at[self.at(o)], dst, zp if sign > 0 else zm)
                if sign > 0:
                    self.plus = cp
                else:
                    self.minus = cp

        def finish(self, out):
            self.plus.wait_recv()
            self.minus.wait_recv()
            t = (self.src[rows_of(0), :] + z_recv[self.at(0), :].astype(F32)
                 + z_recv[self.at(4), :].astype(F32))
            n = self.n
            i, j, m = sem(), sem(), sem()
            f_send[rows_of(n), :] = t
            far = [pltpu.make_async_remote_copy(
                src_ref=f_send.at[rows_of(n), cols_of(q)], dst_ref=f_recv.at[rows_of(2 * n)],
                send_sem=ssem.at[(i, j)[q]], recv_sem=rsem.at[i],
                device_id=(other0, other1)[q], device_id_type=MESH) for q in (0, 1)]
            near = pltpu.make_async_remote_copy(
                src_ref=f_send.at[rows_of(n), cols_of(1 - k)], dst_ref=f_recv.at[rows_of(2 * n + 1)],
                send_sem=ssem.at[m], recv_sem=rsem.at[m], device_id=mate, device_id_type=MESH)

            @pl.when(xl != k)
            def _():
                far[0].start()
                far[1].start()

            @pl.when(xl == k)
            def _():
                near.start()

            def done():
                far[0].wait_recv()

                @pl.when(xl != k)
                def _():
                    near.wait_recv()
                    small[rows_of(n), :] = (
                        f_recv[rows_of(2 * n), :]
                        + f_recv[rows_of(2 * n + 1), :]).astype(BF)
                    far[0].wait_send()
                    far[1].wait_send()

                @pl.when(xl == k)
                def _():
                    small[rows_of(n), :] = (
                        f_recv[rows_of(2 * n), :]
                        + f_send[rows_of(n), cols_of(k)]).astype(BF)
                    near.wait_send()

                return lcopy(small.at[rows_of(n)], out)

            return done

    other_rows = pl.ds(ROWS, ROWS)
    half_rows = pl.ds(0, ROWS)

    def weight_grad(lhs_a, lhs_b, rhs, out, steps, own_off):
        def body(m, _):
            rows = pl.ds(pl.multiple_of(m * 128, 128), 128)
            cols = pl.ds(pl.multiple_of(m * 128 + own_off, 128), 128)
            dims = (((0,), (0,)), ((), ()))
            v = lax.dot_general(lhs_a[half_rows, cols], rhs[half_rows, :], dims, preferred_element_type=F32)
            v = v + lax.dot_general(lhs_b[:, rows], rhs[other_rows, :], dims, preferred_element_type=F32)
            out[rows, :] = v.astype(BF)
            return 0

        lax.fori_loop(0, steps, body, 0)

    gt, gg = Gather(tok, tok_arrived), Gather(grad, grad_arrived)
    gt.step(1)
    own_up.wait()
    w1.wait_recv()
    matmul(tok, up, part.at[0], PLACE[0], False)
    gt.step(2)
    for o in (1, -1):
        matmul(tok, up, part.at[0], PLACE[o], False)
    gt.step(3)
    own_down.wait()
    w2.wait_recv()
    red_p, red_q = Reduce(part.at[0], 0), Reduce(part.at[1], 1)
    for o in (2, -2):
        matmul(tok, up, part.at[0], PLACE[o], False)
    red_p.step1(0)
    gt.step(4)
    gg.step(1)
    for o in (3, -3):
        matmul(tok, up, part.at[0], PLACE[o], False)
    red_p.step2(0)
    gt.finish()
    matmul(tok, up, part.at[0], PLACE[4], False)
    red_p.step1(1)
    gg.step(2)
    matmul(grad, down, part.at[1], PLACE[0], True)
    red_p.step2(1)
    red_p.cross(0)
    for o in (1, -1):
        matmul(grad, down, part.at[1], PLACE[o], True)
    gg.step(3)
    red_p.cross(1)
    red_p.send()
    tok_mate = rcopy(tok.at[:, cols_of(1 - k)], tok_o, mate)
    for o in (2, -2):
        matmul(grad, down, part.at[1], PLACE[o], True)
    gg.step(4)
    red_q.step1(0)
    h = red_p.result()
    hid[rows_of(0), :] = h
    act[rows_of(xh * 4 + y), :] = gelu(h).astype(BF)
    sp_a = Spread(act)
    sp_a.start()
    for o in (3, -3):
        matmul(grad, down, part.at[1], PLACE[o], True)
    red_q.step2(0)
    gg.finish()
    matmul(grad, down, part.at[1], PLACE[4], True)
    sp_a.second()
    red_q.step1(1)
    grad_mate = rcopy(grad.at[:, cols_of(1 - k)], grad_o, mate)
    fa = sp_a.forward(0)
    red_q.step2(1)
    fa += sp_a.forward(1)
    red_q.cross(0)
    red_q.cross(1)
    red_q.send()
    for cp in fa:
        cp.wait_recv()
    act_mate = rcopy(act.at[half_rows], act.at[other_rows], mate)
    zm_ = ZReduce(part.at[0], 0)
    matmul(act, down, part.at[0], PLACE[4], False)
    zm_.step1()
    for o in (3, -3):
        matmul(act, down, part.at[0], PLACE[o], False)
    d = red_q.result()
    hgrad[rows_of(xh * 4 + y), :] = (d * gelu_slope(hid[rows_of(0), :])).astype(BF)
    sp_h = Spread(hgrad)
    sp_h.start()
    zm_.step(3)
    for o in (2, -2):
        matmul(act, down, part.at[0], PLACE[o], False)
    sp_h.second()
    zm_.step(2)
    fh = sp_h.forward(0)
    for o in (1, -1):
        matmul(act, down, part.at[0], PLACE[o], False)
    zm_.step(1)
    fh += sp_h.forward(1)
    matmul(act, down, part.at[0], PLACE[0], False)
    for cp in fh:
        cp.wait_recv()
    zi = ZReduce(part.at[1], 1)
    matmul(hgrad, up, part.at[1], PLACE[4], True)
    zi.step1()
    for o in (3, -3):
        matmul(hgrad, up, part.at[1], PLACE[o], True)
    hg_mate = rcopy(hgrad.at[half_rows], hgrad.at[other_rows], mate)
    done_m = zm_.finish(mixed_out)
    zi.step(3)
    for o in (2, -2):
        matmul(hgrad, up, part.at[1], PLACE[o], True)
    zi.step(2)
    for o in (1, -1):
        matmul(hgrad, up, part.at[1], PLACE[o], True)
    zi.step(1)
    matmul(hgrad, up, part.at[1], PLACE[0], True)
    out_m = done_m()
    tok_mate.wait_recv()
    hg_mate.wait_recv()
    weight_grad(tok, tok_o, hgrad, upg, HALF // 128, k * HALF)
    out_u = lcopy(upg, upg_out)
    done_i = zi.finish(igrad_out)
    grad_mate.wait_recv()
    act_mate.wait_recv()

    def down_body(m, _):
        rows = pl.ds(pl.multiple_of(m * 128, 128), 128)
        dims = (((0,), (0,)), ((), ()))
        v = lax.dot_general(act[half_rows, rows], grad[half_rows, cols_of(k)], dims, preferred_element_type=F32)
        v = v + lax.dot_general(act[other_rows, rows], grad_o[...], dims, preferred_element_type=F32)
        downg[rows, :] = v.astype(BF)
        return 0

    lax.fori_loop(0, WIDE // 128, down_body, 0)
    out_d = lcopy(downg, downg_out)
    out_i = done_i()
    for cp in sends:
        cp.wait_send()
    tok_sent()
    grad_sent()
    for cp in (out_m, out_u, out_d, out_i):
        cp.wait()


def local(tokens, up_weight, down_weight, grad_out):
    vm = pltpu.VMEM
    any_ = pl.BlockSpec(memory_space=pl.ANY)
    return pl.pallas_call(
        kernel,
        name="ffn",
        out_shape=(
            jax.ShapeDtypeStruct((TOK, HALF), BF),
            jax.ShapeDtypeStruct((TOK, HALF), BF),
            jax.ShapeDtypeStruct((HALF, WIDE), BF),
            jax.ShapeDtypeStruct((WIDE, HALF), BF),
        ),
        in_specs=[any_] * 4,
        out_specs=(any_,) * 4,
        scratch_shapes=[
            vm((WIDE, WIDE), BF), vm((WIDE, WIDE), BF),
            vm((ROWS, WIDE), BF), vm((ROWS, WIDE), BF),
            vm((2 * ROWS, WIDE), BF), vm((2 * ROWS, WIDE), BF),
            vm((ROWS, HALF), BF), vm((ROWS, HALF), BF),
            vm((2, ROWS, WIDE), F32),
            vm((2 * TOK, WIDE), F32),
            vm((12 * TOK, WIDE), BF), vm((12 * TOK, WIDE), BF),
            vm((2 * TOK, WIDE), F32), vm((2 * TOK, WIDE), F32),
            vm((16 * TOK, WIDE), BF), vm((16 * TOK, WIDE), BF),
            vm((2 * TOK, WIDE), F32), vm((4 * TOK, HALF), F32),
            vm((HALF, WIDE), BF), vm((WIDE, HALF), BF),
            vm((2 * TOK, HALF), BF),
            pltpu.SemaphoreType.DMA((128,)),
            pltpu.SemaphoreType.DMA((128,)),
            pltpu.SemaphoreType.DMA((16,)),
        ],
        compiler_params=pltpu.CompilerParams(
            collective_id=0, has_side_effects=True, vmem_limit_bytes=60 * 2**20
        ),
        cost_estimate=pl.CostEstimate(flops=12_600_000_000, bytes_accessed=10_000_000, transcendentals=300_000),
    )(tokens, up_weight, down_weight, grad_out)


def solution(mesh):
    placed = (P("col", "row"), P("row", "col"), P("col", "row"), P("col", "row"))
    return jax.shard_map(
        local,
        mesh=mesh,
        in_specs=placed,
        out_specs=(P("col", "row"), P("col", "row"), P("row", "col"), P("col", "row")),
        check_vma=False,
    )
```

time: 637 us -> 151 us (0.24)
  waiting for transfers between devices: 577 us -> 0 us
  Pallas kernels: 0 us -> 141 us
  matrix products: 37.9 us -> 0 us
  between operations: 14.2 us -> 0.64 us
    reduce_scatter x4 -> x0, waiting for transfers between devices: 331 us -> none  [the longest x1 102 us: local(): lax.psum_scatter(jnp.dot(gathered, up_weight, preferred_element_type=jnp....]
    all_gather x4 -> x0, waiting for transfers between devices: 243 us -> none  [the longest x1 74.5 us: local(): cotangent = lax.all_gather(grad_out, 'col', axis=0, tiled=True)]
    pallas_call x0 -> x1, Pallas kernels: none -> 141 us  [local(): pl.pallas_call(kernel, name='ffn', out_shape=(jax.ShapeDtypeStruct((TOK,...]
    dot_general x6 -> x0, matrix products: 37.9 us -> none  [the longest x2 13.8 us: times_trans(): lax.dot_general(left, right, (((1,), (1,)), ((), ())), preferred_element_...]
  transfers between devices with their start and end apart: 8 -> 0, of which waited for: 8 -> 0; matrix products, arithmetic and copies ran while one was open for 7% -> 0% of each run, Pallas kernels for 0% -> 0%
where the time goes in v1:
time: 151 us; the launch traced here: 148 us
  Pallas kernels  141 us (93%)
  local copies, waits for them, and re-layouts  7.08 us (5%)
    pallas_call x1, Pallas kernels, local(): pl.pallas_call(kernel, name='ffn', out_shape=(jax.ShapeDtypeStruct((TOK,...  141 us
    unnamed x6, local copies, waits for them, and re-layouts  7.08 us

profile of v1, /device:TPU:8, one launch (start us, length us, event | category | flops | bytes accessed | tf_op | source)
XLA Modules:
  0.0 148.4 jit_solution(15566812542520799682)
XLA Ops:
  0.6 140.6 %ffn.1 = (bf16[80,640]{1,0:T(8,128)(2,1)}, bf16[80,640]{1,0:T(8,128)(2,1)}, bf16[640,1280]{1,0:T(8,128)(2,1)}, bf16[1280,640]{1,0:T(8,128)(2,1)}) custom-call(bf16[80,640]{1,0:T(8,128)(2,1)} %tok_in.1, bf16[640,1280]{1,0:T(8,128)(2,1)} %up_in.1, bf16[1280,640]{1,0:T(8,128)(2,1)} %down_in.1, bf16[80,640]{1,0:T(8,128)(2,1)} %grad_in.1), custom_call_target="tpu_custom_call" | custom-call | flops 12600000512 | bytes 10000000 | tf_op jit(solution)/shard_map/ffn/pallas_call | solution.py:510
  141.3 1.5 %copy.12 = bf16[80,640]{1,0:T(8,128)(2,1)} copy(bf16[80,640]{1,0:T(8,128)(2,1)} %get-tuple-element.8) | data formatting | bytes 204800
  142.8 1.5 %copy.13 = bf16[80,640]{1,0:T(8,128)(2,1)} copy(bf16[80,640]{1,0:T(8,128)(2,1)} %get-tuple-element.9) | data formatting | bytes 204800
  144.4 0.0 copy-start
  144.4 2.8 %copy.14 = bf16[640,1280]{1,0:T(8,128)(2,1)} copy(bf16[640,1280]{1,0:T(8,128)(2,1)} %get-tuple-element.10) | data formatting | bytes 3276800
  147.2 0.0 copy-done
  147.2 1.2 copy.15
Async XLA Ops:
  144.4 2.8 %copy-start = (bf16[1280,640]{1,0:T(8,128)(2,1)S(1)}, bf16[1280,640]{1,0:T(8,128)(2,1)}, u32[]{:S(2)}) copy-start(bf16[1280,640]{1,0:T(8,128)(2,1)} %get-tuple-element.11) | copy-start | bytes 4915204

commit v2 on v0

v2 whole, which is shorter than its diff:
```python
import jax
import jax.numpy as jnp
from jax import lax
from jax.experimental import pallas as pl
from jax.experimental.pallas import tpu as pltpu
from jax.sharding import PartitionSpec as P

MESH = pl.DeviceIdType.MESH
BF = jnp.bfloat16
F32 = jnp.float32

TOK = 80
HALF = 640
WIDE = 1280
ROWS = 8 * TOK

PLACE = {0: 0, 1: 1, -1: 2, 2: 3, -2: 4, 3: 5, -3: 6, 4: 7}
SPAN = ((0, 1), (1, 2), (3, 2), (5, 2), (7, 1))
SUB = ((0, 48), (48, 32))

C0 = 0.7978845608028654
C1 = 0.044715

ORDER = (
    "W2s", "W1s", "Gs", "Tzp0", "Tzm0", "D", "Tzp1", "Tzm1", "Q0", "Qx0", "Tzp2", "Tzm2",
    "P0", "Px0", "U", "Tzp3", "Tzm3", "P1", "Px2", "Tzp4", "Tzm4", "Px1", "Tzp5", "P2",
    "Tzm5", "Px4", "Tzp6", "Tzm6", "Px3", "Gzp0", "Gzm1", "P3", "Gzp1", "Px5", "Gzm0", "Px6",
    "P4", "Tm", "Py0pa", "Py0ma", "Gzp2", "Py0mb", "Py0pb", "Px7", "Gzm3", "Gzp3", "Gzm2", "Q1",
    "Py0mc", "Py0pc", "Qx1", "Gzp4", "Gzm5", "Qx2", "Gzp5", "Py1pa", "Py1ma", "Py1pb", "Gzm4", "Q2",
    "Pe0", "Gzp6", "Qx4", "Py1pc", "Py1mb", "Py1mc", "Gzm6", "Q3", "Qx5", "Pf0p", "Qx6", "Pn0",
    "Q4", "Pe1", "Gm", "Qx7", "Pf0m", "Qx3", "Pf1p", "Pn1", "M0", "M1", "Qy1ma", "Qy1pb",
    "Qy1mb", "Qy1pa", "Qy0ma", "Qy0pa", "Pf1m", "Qy0pb", "Qy1mc", "Qy1pc", "Qy0mc", "Qy0mb", "Qy0pc", "M4",
    "Mrp0", "Mrm0", "Qe1", "M3", "Mrp1", "Mrm1", "Qe0", "M2", "Am", "Mrp2", "Mrm2", "Qf1p",
    "Qn1", "Mrp3", "Mrm3", "Qn0", "Mrp4", "Mrm4", "DG0", "DG1", "Qf1m", "Qf0p", "Mrp5", "Mrm5",
    "DG2", "DG3", "Qf0m", "Mrp6", "Mrm6", "I4", "Irm0", "I3", "Irp1", "Irm1", "I2", "Irp0",
    "I1", "I0", "Hm", "Irm2", "Mt1", "Irp3", "Mt0", "Irm3", "Irp2", "Irm4", "UG0", "Irp5",
    "UG1", "Irp4", "Mo", "Irm5", "Irm6", "Irp6", "It1", "It0", "Io",
)


def gelu(v):
    return 0.5 * v * (1.0 + jnp.tanh(C0 * (v + C1 * v * v * v)))


def gelu_slope(v):
    t = jnp.tanh(C0 * (v + C1 * v * v * v))
    return 0.5 * (1.0 + t) + 0.5 * v * (1.0 - t * t) * (C0 * (1.0 + 3.0 * C1 * v * v))


def rows_of(place, many=1):
    if isinstance(place, int):
        return pl.ds(place * TOK, many * TOK)
    return pl.ds(pl.multiple_of(place * TOK, TOK), many * TOK)


def cols_of(half):
    if isinstance(half, int):
        return pl.ds(half * HALF, HALF)
    return pl.ds(pl.multiple_of(half * HALF, HALF), HALF)


def kernel(
    tok_in, up_in, down_in, grad_in,
    mixed_out, igrad_out, upg_out, downg_out,
    up, down, up_t, down_t, tok, grad, act, hgrad, tok_o, grad_o,
    part, hid, x_send, x_recv, y_send, y_recv, z_send, z_recv, f_send, f_recv,
    upg, downg, small,
    ssem, rsem, lsem,
):
    r, c = lax.axis_index("row"), lax.axis_index("col")
    y, xh, k = r // 4, (r // 2) % 2, r % 2
    xl, z = c // 8, c % 8

    def row_id(yy, hh, kk):
        return (yy * 2 + hh) * 2 + kk

    mate = (row_id(y, xh, 1 - k), c)
    yside = {"p": (row_id((y + 1) % 4, xh, k), c), "m": (row_id((y + 3) % 4, xh, k), c)}
    across = (row_id(y, 1 - xh, k), c)
    zside = {"p": (r, xl * 8 + (z + 1) % 8), "m": (r, xl * 8 + (z + 7) % 8)}
    other_c = (1 - xl) * 8 + z
    other = ((row_id(y, xh, 0), other_c), (row_id(y, xh, 1), other_c))

    count = [0, 0]
    ends = []
    msg = {}

    def sem():
        count[0] += 1
        return count[0] - 1

    def remote(src, dst, dev):
        i = sem()
        return pltpu.make_async_remote_copy(
            src_ref=src, dst_ref=dst, send_sem=ssem.at[i], recv_sem=rsem.at[i],
            device_id=dev, device_id_type=MESH,
        )

    def send(name, src, dst, dev):
        cp = remote(src, dst, dev)
        cp.start()
        ends.append(cp.wait_send)
        msg[name] = cp.wait_recv

    def got(*names):
        for name in names:
            wait = msg[name]
            if wait is not None:
                wait()
                msg[name] = None

    def lcopy(src, dst):
        cp = pltpu.make_async_copy(src, dst, lsem.at[count[1]])
        count[1] += 1
        cp.start()
        return cp.wait

    def unless(cond, f):
        def g():
            pl.when(cond)(f)

        return g

    own_rows = pl.ds(pl.multiple_of(k * HALF, HALF), HALF)
    msg["up"] = lcopy(up_in, up.at[own_rows])
    msg["down"] = lcopy(down_in, down.at[:, cols_of(k)])

    barrier = pltpu.get_barrier_semaphore()
    for dev in (mate, *yside.values(), across, *zside.values(), *other):
        pl.semaphore_signal(barrier, inc=1, device_id=dev, device_id_type=MESH)
    pl.semaphore_wait(barrier, 8)

    def spread(name, src, buf):
        i, j = sem(), sem()
        dst = buf.at[k, rows_of(0)]
        far = pltpu.make_async_remote_copy(
            src_ref=src, dst_ref=dst, send_sem=ssem.at[i], recv_sem=rsem.at[i + k],
            device_id=(row_id(y, xh, xl), other_c), device_id_type=MESH,
        )
        near = pltpu.make_async_remote_copy(
            src_ref=src, dst_ref=dst, send_sem=ssem.at[j], recv_sem=rsem.at[i + k],
            device_id=mate, device_id_type=MESH,
        )
        stay = pltpu.make_async_copy(src, dst, rsem.at[i + k])
        far.start()
        pl.when(k != xl)(near.start)
        pl.when(k == xl)(stay.start)
        ends.append(far.wait_send)
        ends.append(unless(k != xl, near.wait_send))
        for h in (0, 1):
            msg[f"{name}s{h}"] = pltpu.make_async_copy(src, buf.at[h, rows_of(0)], rsem.at[i + h]).wait

    spread("T", tok_in, tok)

    tasks = {}
    tasks["W1s"] = lambda: send("W1", up_in, up.at[own_rows], mate)
    tasks["W2s"] = lambda: send("W2", down_in, down.at[:, cols_of(k)], mate)
    tasks["Gs"] = lambda: spread("G", grad_in, grad)

    def gather(name, buf):
        def source(off, h):
            if off == 0:
                return f"{name}s{h}"
            if off == 4:
                return f"{name}zp6" if h == 0 else f"{name}zm6"
            d, first = ("p", 0) if off < 0 else ("m", 1)
            return f"{name}z{d}{2 * (abs(off) - 1) + (0 if h == first else 1)}"

        def step(d, i):
            n, first, sign = i // 2, 0 if d == "p" else 1, -1 if d == "p" else 1
            h = first if i % 2 == 0 else 1 - first
            off, to = sign * n, sign * (n + 1)
            got(source(off, h))
            send(f"{name}z{d}{i}", buf.at[h, rows_of(PLACE[off])],
                 buf.at[h, rows_of(PLACE[4 if to == -4 else to])], zside[d])

        for d in "pm":
            for i in range(7):
                tasks[f"{name}z{d}{i}"] = lambda d=d, i=i: step(d, i)
        return source

    tok_source, grad_source = gather("T", tok), gather("G", grad)

    def product(lhs, rhs, out, i):
        first, many = SPAN[i]
        rows = rows_of(first, many)
        v = (
            jnp.dot(lhs[0, rows, :], rhs[pl.ds(0, HALF), :], preferred_element_type=F32)
            + jnp.dot(lhs[1, rows, :], rhs[pl.ds(HALF, HALF), :], preferred_element_type=F32))
        out[0, rows, :] = v[:, :HALF]
        out[1, rows, :] = v[:, HALF:]

    def turn(src, dst):
        def body(n, _):
            cols = pl.ds(pl.multiple_of(n * 256, 256), 256)
            dst[:, cols] = src[cols, :].T
            return 0

        lax.fori_loop(0, WIDE // 256, body, 0)

    def turn_up():
        got("up", "W1")
        turn(up, up_t)

    def turn_down():
        got("down", "W2")
        turn(down, down_t)

    tasks["U"], tasks["D"] = turn_up, turn_down

    def offs(i):
        return (i,) if i in (0, 4) else (i, -i)

    def way(n, R, source, lhs, rhs, N, lhs2, rhs2, finish):
        src = part.at[n]

        def first(i):
            got("up", "W1", *(source(o, h) for o in offs(i) for h in (0, 1)))
            product(lhs, rhs, src, i)

        for i in range(5):
            tasks[f"{R}{i}"] = lambda i=i: first(i)

        def xbuf(p):
            return rows_of(n * 8 + p) if isinstance(p, int) else pl.ds(pl.multiple_of((n * 8 + p) * TOK, TOK), TOK)

        def xstep(p):
            x_send[xbuf(p), :] = src[1 - xh, rows_of(p), :].astype(BF)
            send(f"{R}x{p}", x_send.at[xbuf(p)], x_recv.at[xbuf(p)], across)

        def paired(p, r):
            start, many = SUB[r]
            rows = pl.ds(pl.multiple_of(p * TOK + start, 16), many)
            far = pl.ds(pl.multiple_of((n * 8 + p) * TOK + start, 16), many)
            return src[xh, rows, :] + x_recv[far, :].astype(F32)

        def ybuf(b, d, s, r):
            return pl.ds(((n * 2 + b) * 6 + "pm".index(d) * 3 + "abc".index(s)) * SUB[0][1], SUB[r][1])

        def ystep(b, d, s):
            got(*(f"{R}x{b * 4 + i}" for i in range(4)))
            near = 1 if d == "p" else 3
            r = b if d == "p" else 1 - b
            if s == "b":
                r = 1 - r
            v = paired(b * 4 + (y + (2 if s == "a" else near)) % 4, r)
            if s == "c":
                got(f"{R}y{b}{d}a")
                v = v + y_recv[ybuf(b, d, "a", r), :].astype(F32)
            mine = ybuf(b, d, s, r)
            y_send[mine, :] = v.astype(BF)
            send(f"{R}y{b}{d}{s}", y_send.at[mine], y_recv.at[mine], yside[d])

        def piece(b, yy, h):
            return lhs2.at[h, rows_of(b * 4 + yy)]

        def estep(b):
            got(*(f"{R}y{b}{d}{s}" for d in "pm" for s in "bc"))
            for r in (0, 1):
                p, m = ("c", "b") if r == b else ("b", "c")
                v = (paired(b * 4 + y, r) + y_recv[ybuf(b, "p", p, r), :].astype(F32)
                     + y_recv[ybuf(b, "m", m, r), :].astype(F32))
                start, many = SUB[r]
                v = finish(v, pl.ds(b * TOK + start, many)).astype(BF)
                lhs2[xh, pl.ds(pl.multiple_of((b * 4 + y) * TOK + start, 16), many), :] = v
            mine = piece(b, y, xh)
            for d in "pm":
                send(f"{R}o{b}{d}", mine, mine, yside[d])
            send(f"{R}a{b}", mine, mine, across)

        def nstep(b):
            got(f"{R}a{b}")
            theirs = piece(b, y, 1 - xh)
            for d in "pm":
                send(f"{R}n{b}{d}", theirs, theirs, yside[d])

        def fstep(b, d):
            if d == "p":
                got(f"{R}o{b}p")
                p = piece(b, (y + 3) % 4, xh)
            else:
                got(f"{R}n{b}m")
                p = piece(b, (y + 1) % 4, 1 - xh)
            send(f"{R}f{b}{d}", p, p, yside[d])

        for p in range(8):
            tasks[f"{R}x{p}"] = lambda p=p: xstep(p)
        for b in (0, 1):
            for d in "pm":
                for s in "abc":
                    tasks[f"{R}y{b}{d}{s}"] = lambda b=b, d=d, s=s: ystep(b, d, s)
                tasks[f"{R}f{b}{d}"] = lambda b=b, d=d: fstep(b, d)
            tasks[f"{R}e{b}"] = lambda b=b: estep(b)
            tasks[f"{R}n{b}"] = lambda b=b: nstep(b)

        def second(i):
            for b in {0: (0,), 1: (0,), 2: (0, 1), 3: (1,), 4: (1,)}[i]:
                got(*(f"{R}{q}{b}{d}" for q in "onf" for d in "pm"))
            got("down", "W2")
            product(lhs2, rhs2, src, i)

        for i in range(5):
            tasks[f"{N}{i}"] = lambda i=i: second(i)

        def zbuf(d, i):
            return rows_of(n * 14 + "pm".index(d) * 7 + i)

        def zstep(d, i):
            first = 0 if d == "p" else 1
            h = first if i % 2 == 0 else 1 - first
            o = 4 - (i + 1) // 2
            place = PLACE[o if d == "p" or o == 4 else -o]
            v = src[h, rows_of(place), :]
            if i >= 2:
                got(f"{N}r{d}{i - 2}")
                v = v + z_recv[zbuf(d, i - 2), :].astype(F32)
            z_send[zbuf(d, i), :] = v.astype(BF)
            send(f"{N}r{d}{i}", z_send.at[zbuf(d, i)], z_recv.at[zbuf(d, i)], zside[d])

        for d in "pm":
            for i in range(7):
                tasks[f"{N}r{d}{i}"] = lambda d=d, i=i: zstep(d, i)

        def tstep(h):
            p, m = (6, 5) if h == 0 else (5, 6)
            got(f"{N}rp{p}", f"{N}rm{m}")
            mine = rows_of(n * 2 + h)
            f_send[mine, :] = (src[h, rows_of(0), :] + z_recv[zbuf("p", p), :].astype(F32)
                               + z_recv[zbuf("m", m), :].astype(F32))
            if f"{N}far" not in msg:
                msg[f"{N}far"], msg[f"{N}near"] = sem(), sem()
            i, j = msg[f"{N}far"], msg[f"{N}near"]
            far = pltpu.make_async_remote_copy(
                src_ref=f_send.at[mine], dst_ref=f_recv.at[rows_of(2 * n)],
                send_sem=ssem.at[i if h == 0 else sem()], recv_sem=rsem.at[i],
                device_id=other[h], device_id_type=MESH)
            near = pltpu.make_async_remote_copy(
                src_ref=f_send.at[mine], dst_ref=f_recv.at[rows_of(2 * n + 1)],
                send_sem=ssem.at[j], recv_sem=rsem.at[j], device_id=mate, device_id_type=MESH)
            pl.when(xl != k)(far.start)
            give = jnp.logical_and(xl == k, k != h)
            pl.when(give)(near.start)
            ends.append(unless(xl != k, far.wait_send))
            ends.append(unless(give, near.wait_send))
            msg[f"{N}o"] = (far.wait_recv, near.wait_recv)

        def ostep():
            far, near = msg[f"{N}o"]
            far()
            mine = rows_of(n)

            @pl.when(xl != k)
            def _():
                near()
                small[mine, :] = (f_recv[rows_of(2 * n), :] + f_recv[rows_of(2 * n + 1), :]).astype(BF)

            @pl.when(xl == k)
            def _():
                small[mine, :] = (f_recv[rows_of(2 * n), :] + f_send[rows_of(n * 2 + k), :]).astype(BF)

            ends.append(lcopy(small.at[mine], (mixed_out, igrad_out)[n]))

        tasks[f"{N}t0"], tasks[f"{N}t1"], tasks[f"{N}o"] = lambda: tstep(0), lambda: tstep(1), ostep

    def forward(v, rows):
        hid[rows, :] = v
        return gelu(v)

    def backward(v, rows):
        return v * gelu_slope(hid[rows, :])

    way(0, "P", tok_source, tok, up, "M", act, down, forward)
    way(1, "Q", grad_source, grad, down_t, "I", hgrad, up_t, backward)

    low, high = pl.ds(0, ROWS), pl.ds(ROWS, ROWS)

    def swap(name, source, buf, out):
        got(*(source(o, h) for o in PLACE for h in (0, 1)))
        send(name, buf.at[1 - k], out, mate)

    tasks["Tm"] = lambda: swap("Tm", tok_source, tok, tok_o)
    tasks["Gm"] = lambda: swap("Gm", grad_source, grad, grad_o)

    def twin(name, buf):
        for h in (0, 1):
            send(f"{name}{h}", buf.at[h, low], buf.at[h, high], mate)

    tasks["Am"] = lambda: twin("Am", act)
    tasks["Hm"] = lambda: twin("Hm", hgrad)

    def outer(a, b):
        return lax.dot_general(a, b, (((0,), (0,)), ((), ())), preferred_element_type=F32)

    def dg(i):
        got("Gm", "Am0", "Am1")
        for h, first, many in (((0, 0, 256),), ((0, 256, 384),), ((1, 0, 256),), ((1, 256, 384),))[i]:
            cols, rows = pl.ds(first, many), pl.ds(h * HALF + first, many)
            v = outer(act[h, low, cols], grad[k]) + outer(act[h, high, cols], grad_o[...])
            downg[rows, :] = v.astype(BF)
            ends.append(lcopy(downg.at[rows], downg_out.at[rows]))

    def ug(i):
        got("Tm", "Hm0", "Hm1")
        rows = pl.ds(*((0, 256), (256, 384))[i])
        for h in (0, 1):
            v = outer(tok[k, :, rows], hgrad[h, low, :]) + outer(tok_o[:, rows], hgrad[h, high, :])
            upg[rows, cols_of(h)] = v.astype(BF)
        ends.append(lcopy(upg.at[rows], upg_out.at[rows]))

    for i in range(4):
        tasks[f"DG{i}"] = lambda i=i: dg(i)
    for i in range(2):
        tasks[f"UG{i}"] = lambda i=i: ug(i)

    for name in ORDER[:-1]:
        tasks[name]()
    for end in ends:
        end()
    ends.clear()
    tasks[ORDER[-1]]()
    for end in ends:
        end()


CUTS = 4


def hand_on(a, b, c, d, a_out, b_out, c_out, d_out, a_mid, b_mid, c_mid, d_mid, in_sem, out_sem):
    ins, outs = [], []
    for src, mid, dst, many in ((c, c_mid, c_out, CUTS), (d, d_mid, d_out, CUTS), (a, a_mid, a_out, 1), (b, b_mid, b_out, 1)):
        rows = src.shape[0] // many
        for i in range(many):
            part = pl.ds(i * rows, rows)
            n = len(ins)
            ins.append(pltpu.make_async_copy(src.at[part], mid.at[part], in_sem.at[n]))
            outs.append(pltpu.make_async_copy(mid.at[part], dst.at[part], out_sem.at[n]))
            ins[n].start()
    for first, then in zip(ins, outs):
        first.wait()
        then.start()
    for cp in outs:
        cp.wait()


def local(tokens, up_weight, down_weight, grad_out):
    vm = pltpu.VMEM
    any_ = pl.BlockSpec(memory_space=pl.ANY)
    done = pl.pallas_call(
        kernel,
        name="ffn",
        out_shape=(
            jax.ShapeDtypeStruct((TOK, HALF), BF),
            jax.ShapeDtypeStruct((TOK, HALF), BF),
            jax.ShapeDtypeStruct((HALF, WIDE), BF),
            jax.ShapeDtypeStruct((WIDE, HALF), BF),
        ),
        in_specs=[any_] * 4,
        out_specs=(any_,) * 4,
        scratch_shapes=[
            vm((WIDE, WIDE), BF), vm((WIDE, WIDE), BF),
            vm((WIDE, WIDE), BF), vm((WIDE, WIDE), BF),
            vm((2, ROWS, HALF), BF), vm((2, ROWS, HALF), BF),
            vm((2, 2 * ROWS, HALF), BF), vm((2, 2 * ROWS, HALF), BF),
            vm((ROWS, HALF), BF), vm((ROWS, HALF), BF),
            vm((2, 2, ROWS, HALF), F32),
            vm((2 * TOK, HALF), F32),
            vm((16 * TOK, HALF), BF), vm((16 * TOK, HALF), BF),
            vm((24 * 48, HALF), BF), vm((24 * 48, HALF), BF),
            vm((28 * TOK, HALF), BF), vm((28 * TOK, HALF), BF),
            vm((4 * TOK, HALF), F32), vm((4 * TOK, HALF), F32),
            vm((HALF, WIDE), BF), vm((WIDE, HALF), BF),
            vm((2 * TOK, HALF), BF),
            pltpu.SemaphoreType.DMA((160,)),
            pltpu.SemaphoreType.DMA((160,)),
            pltpu.SemaphoreType.DMA((16,)),
        ],
        compiler_params=pltpu.CompilerParams(
            collective_id=0, has_side_effects=True, vmem_limit_bytes=60 * 2**20
        ),
        cost_estimate=pl.CostEstimate(flops=12_600_000_000, bytes_accessed=10_000_000, transcendentals=300_000),
    )(tokens, up_weight, down_weight, grad_out)
    return pl.pallas_call(
        hand_on,
        name="hand_on",
        out_shape=[jax.ShapeDtypeStruct(x.shape, x.dtype) for x in done],
        in_specs=[any_] * 4,
        out_specs=[any_] * 4,
        scratch_shapes=[pltpu.VMEM(x.shape, x.dtype) for x in done]
        + [pltpu.SemaphoreType.DMA((2 * CUTS + 2,))] * 2,
        cost_estimate=pl.CostEstimate(flops=0, bytes_accessed=8_000_000, transcendentals=0),
    )(*done)


def solution(mesh):
    placed = (P("col", "row"), P("row", "col"), P("col", "row"), P("col", "row"))
    return jax.shard_map(
        local,
        mesh=mesh,
        in_specs=placed,
        out_specs=(P("col", "row"), P("col", "row"), P("row", "col"), P("col", "row")),
        check_vma=False,
    )
```

time: 637 us -> 116 us (0.18)
  waiting for transfers between devices: 577 us -> 0 us
  Pallas kernels: 0 us -> 114 us
  matrix products: 37.9 us -> 0 us
  between operations: 14.2 us -> 0.8 us
    reduce_scatter x4 -> x0, waiting for transfers between devices: 331 us -> none  [the longest x1 102 us: local(): lax.psum_scatter(jnp.dot(gathered, up_weight, preferred_element_type=jnp....]
    all_gather x4 -> x0, waiting for transfers between devices: 243 us -> none  [the longest x1 74.5 us: local(): cotangent = lax.all_gather(grad_out, 'col', axis=0, tiled=True)]
    pallas_call x0 -> x2, Pallas kernels: none -> 114 us  [the longest x1 111 us: local(): pl.pallas_call(kernel, name='ffn', out_shape=(jax.ShapeDtypeStruct((TOK,...]
    dot_general x6 -> x0, matrix products: 37.9 us -> none  [the longest x2 13.8 us: times_trans(): lax.dot_general(left, right, (((1,), (1,)), ((), ())), preferred_element_...]
  transfers between devices with their start and end apart: 8 -> 0, of which waited for: 8 -> 0; matrix products, arithmetic and copies ran while one was open for 7% -> 0% of each run, Pallas kernels for 0% -> 0%
where the time goes in v2:
time: 116 us; the launch traced here: 115 us
  Pallas kernels  114 us (98%)
    pallas_call x1, Pallas kernels, local(): pl.pallas_call(kernel, name='ffn', out_shape=(jax.ShapeDtypeStruct((TOK,...  111 us
    pallas_call x1, Pallas kernels, local(): pl.pallas_call(hand_on, name='hand_on', out_shape=[jax.ShapeDtypeStruct(x...  2.93 us

profile of v2, /device:TPU:8, one launch (start us, length us, event | category | flops | bytes accessed | tf_op | source)
XLA Modules:
  0.0 115.1 jit_solution(15696689419379129175)
XLA Ops:
  0.6 111.4 %ffn.1 = (bf16[80,640]{1,0:T(8,128)(2,1)}, bf16[80,640]{1,0:T(8,128)(2,1)}, bf16[640,1280]{1,0:T(8,128)(2,1)}, bf16[1280,640]{1,0:T(8,128)(2,1)}) custom-call(bf16[80,640]{1,0:T(8,128)(2,1)} %tok_in.1, bf16[640,1280]{1,0:T(8,128)(2,1)} %up_in.1, bf16[1280,640]{1,0:T(8,128)(2,1)} %down_in.1, bf16[80,640]{1,0:T(8,128)(2,1)} %grad_in.1), custom_call_target="tpu_custom_call" | custom-call | flops 12600000512 | bytes 10000000 | tf_op jit(solution)/shard_map/ffn/pallas_call | solution.py:448
  112.0 2.9 %hand_on.1 = (bf16[80,640]{1,0:T(8,128)(2,1)}, bf16[80,640]{1,0:T(8,128)(2,1)}, bf16[640,1280]{1,0:T(8,128)(2,1)}, bf16[1280,640]{1,0:T(8,128)(2,1)}) custom-call(bf16[80,640]{1,0:T(8,128)(2,1)} %get-tuple-element.8.a, bf16[80,640]{1,0:T(8,128)(2,1)} %get-tuple-element.9.b, bf16[640,1280]{1,0:T(8,128)(2,1)} %get-tuple-element.10.c, ...), custom_call_target="tpu_custom_call" | custom-call | bytes 8000000 | tf_op jit(solution)/shard_map/hand_on/pallas_call | solution.py:482

commit v3 on v2

--- a/solution.py
+++ b/solution.py
@@ -22,19 +22,18 @@
 C1 = 0.044715
 
 ORDER = (
-    "W2s", "W1s", "Gs", "Tzp0", "Tzm0", "D", "Tzp1", "Tzm1", "Q0", "Qx0", "Tzp2", "Tzm2",
-    "P0", "Px0", "U", "Tzp3", "Tzm3", "P1", "Px2", "Tzp4", "Tzm4", "Px1", "Tzp5", "P2",
-    "Tzm5", "Px4", "Tzp6", "Tzm6", "Px3", "Gzp0", "Gzm1", "P3", "Gzp1", "Px5", "Gzm0", "Px6",
-    "P4", "Tm", "Py0pa", "Py0ma", "Gzp2", "Py0mb", "Py0pb", "Px7", "Gzm3", "Gzp3", "Gzm2", "Q1",
-    "Py0mc", "Py0pc", "Qx1", "Gzp4", "Gzm5", "Qx2", "Gzp5", "Py1pa", "Py1ma", "Py1pb", "Gzm4", "Q2",
-    "Pe0", "Gzp6", "Qx4", "Py1pc", "Py1mb", "Py1mc", "Gzm6", "Q3", "Qx5", "Pf0p", "Qx6", "Pn0",
-    "Q4", "Pe1", "Gm", "Qx7", "Pf0m", "Qx3", "Pf1p", "Pn1", "M0", "M1", "Qy1ma", "Qy1pb",
-    "Qy1mb", "Qy1pa", "Qy0ma", "Qy0pa", "Pf1m", "Qy0pb", "Qy1mc", "Qy1pc", "Qy0mc", "Qy0mb", "Qy0pc", "M4",
-    "Mrp0", "Mrm0", "Qe1", "M3", "Mrp1", "Mrm1", "Qe0", "M2", "Am", "Mrp2", "Mrm2", "Qf1p",
-    "Qn1", "Mrp3", "Mrm3", "Qn0", "Mrp4", "Mrm4", "DG0", "DG1", "Qf1m", "Qf0p", "Mrp5", "Mrm5",
-    "DG2", "DG3", "Qf0m", "Mrp6", "Mrm6", "I4", "Irm0", "I3", "Irp1", "Irm1", "I2", "Irp0",
-    "I1", "I0", "Hm", "Irm2", "Mt1", "Irp3", "Mt0", "Irm3", "Irp2", "Irm4", "UG0", "Irp5",
-    "UG1", "Irp4", "Mo", "Irm5", "Irm6", "Irp6", "It1", "It0", "Io",
+    "Gs", "W1s", "W2s", "Tzp2", "Tzm2", "P1", "Tzm3", "Gzm2", "Tzp3", "P0", "D", "Gzp3",
+    "Tzp4", "Tzm4", "Gzm3", "Gzp2", "Q1", "Tzp5", "P2", "Qx2", "Py0pa", "Py0ma", "Qx1", "Tzm5",
+    "Py0pb", "Tzp6", "Tzm6", "Q0", "Py0mb", "Qx0", "Gzm4", "Gzp4", "Gzp5", "Q2", "Py0pc", "Py0mc",
+    "Gzm5", "Qx4", "P3", "Qx3", "P4", "Py1pa", "Gzm6", "Py1ma", "Gzp6", "Py1pb", "Px01", "Py1mb",
+    "Q3", "Qx6", "Py1pc", "Qx5", "Py1mc", "Qy0pa", "Q4", "Qy0ma", "Qx7", "Pe01", "Px10", "Qy0mb",
+    "Gm", "Qy0mc", "Px11", "Qy0pc", "Qy0pb", "Qy1mb", "Qy1pb", "Qy1ma", "Px00", "Qy1pa", "Pe10", "Pe11",
+    "Qy1pc", "Qy1mc", "U", "Tm", "Pf1p", "Pf1m", "Pf0m", "Pe00", "Qe1", "M4", "Mrp0", "Mrm0",
+    "Pf0p", "M3", "Mrp1", "Mrm1", "Qn1", "Qe0", "Qf1p", "Mrp2", "Mrm2", "M2", "Mrp3", "Mrm3",
+    "Qf1m", "Am", "Qn0", "Mrp4", "Mrm4", "M1", "Mrp5", "Mrm5", "I4", "Irp0", "Irm0", "Qf0p",
+    "I3", "Qf0m", "Irm1", "Irp1", "M0", "DG3", "Irp2", "Irm2", "Mrp6", "I2", "Irm3", "I1",
+    "Mw", "Irp4", "Irm4", "I0", "Irp3", "Mrm6", "DG1", "Hm", "Iw", "Irm5", "Irp6", "DG0",
+    "Irm6", "Irp5", "Mt0", "Mt1", "DG2", "UG0", "Mo", "It0", "It1", "UG1", "Io",
 )
 
 
@@ -63,7 +62,7 @@
     tok_in, up_in, down_in, grad_in,
     mixed_out, igrad_out, upg_out, downg_out,
     up, down, up_t, down_t, tok, grad, act, hgrad, tok_o, grad_o,
-    part, hid, x_send, x_recv, y_send, y_recv, z_send, z_recv, f_send, f_recv,
+    part, hid, h_send, h_recv, x_send, x_recv, y_send, y_recv, z_send, z_recv, s_recv, w_send, w_recv, f_send, f_recv,
     upg, downg, small,
     ssem, rsem, lsem,
 ):
@@ -80,6 +79,9 @@
     zside = {"p": (r, xl * 8 + (z + 1) % 8), "m": (r, xl * 8 + (z + 7) % 8)}
     other_c = (1 - xl) * 8 + z
     other = ((row_id(y, xh, 0), other_c), (row_id(y, xh, 1), other_c))
+    zstep_of = {"p": (z + 1) % 8, "m": (z + 7) % 8}
+    slant = {d: (r, (1 - xl) * 8 + zstep_of[d]) for d in "pm"}
+    givers = [(row_id(y, xh, q), k * 8 + zstep_of[d]) for d in "pm" for q in (0, 1)]
 
     count = [0, 0]
     ends = []
@@ -126,29 +128,46 @@
     msg["down"] = lcopy(down_in, down.at[:, cols_of(k)])
 
     barrier = pltpu.get_barrier_semaphore()
-    for dev in (mate, *yside.values(), across, *zside.values(), *other):
+    for dev in (mate, *yside.values(), across, *zside.values(), *other, *slant.values(), *givers):
         pl.semaphore_signal(barrier, inc=1, device_id=dev, device_id_type=MESH)
-    pl.semaphore_wait(barrier, 8)
+    pl.semaphore_wait(barrier, 14)
 
     def spread(name, src, buf):
-        i, j = sem(), sem()
-        dst = buf.at[k, rows_of(0)]
-        far = pltpu.make_async_remote_copy(
-            src_ref=src, dst_ref=dst, send_sem=ssem.at[i], recv_sem=rsem.at[i + k],
-            device_id=(row_id(y, xh, xl), other_c), device_id_type=MESH,
-        )
-        near = pltpu.make_async_remote_copy(
-            src_ref=src, dst_ref=dst, send_sem=ssem.at[j], recv_sem=rsem.at[i + k],
-            device_id=mate, device_id_type=MESH,
-        )
-        stay = pltpu.make_async_copy(src, dst, rsem.at[i + k])
+        def to(place, col, core, i):
+            j = sem()
+            cp = pltpu.make_async_remote_copy(
+                src_ref=src, dst_ref=buf.at[k, rows_of(place)], send_sem=ssem.at[j], recv_sem=rsem.at[i + k],
+                device_id=(core, col), device_id_type=MESH,
+            )
+            return cp
+
+        def arrived(place, i, h):
+            return pltpu.make_async_copy(src, buf.at[h, rows_of(place)], rsem.at[i + h]).wait
+
+        target = row_id(y, xh, xl)
+        for straight in (True, False):
+            for d in "pm":
+                place = PLACE[-1 if d == "p" else 1]
+                if straight:
+                    msg[name + d] = sem(), sem()
+                i = msg[name + d][0]
+                cp = to(place, (xl if straight else 1 - xl) * 8 + zstep_of[d], target, i)
+                cp.start()
+                ends.append(cp.wait_send)
+                if not straight:
+                    for h in (0, 1):
+                        msg[f"{name}z{d}{h if d == 'p' else 1 - h}"] = arrived(place, i, h)
+        i, _ = sem(), sem()
+        far = to(0, other_c, target, i)
+        near = to(0, c, row_id(y, xh, 1 - k), i)
+        stay = pltpu.make_async_copy(src, buf.at[k, rows_of(0)], rsem.at[i + k])
         far.start()
         pl.when(k != xl)(near.start)
         pl.when(k == xl)(stay.start)
         ends.append(far.wait_send)
         ends.append(unless(k != xl, near.wait_send))
         for h in (0, 1):
-            msg[f"{name}s{h}"] = pltpu.make_async_copy(src, buf.at[h, rows_of(0)], rsem.at[i + h]).wait
+            msg[f"{name}s{h}"] = arrived(0, i, h)
 
     spread("T", tok_in, tok)
 
@@ -175,7 +194,7 @@
                  buf.at[h, rows_of(PLACE[4 if to == -4 else to])], zside[d])
 
         for d in "pm":
-            for i in range(7):
+            for i in range(2, 7):
                 tasks[f"{name}z{d}{i}"] = lambda d=d, i=i: step(d, i)
         return source
 
@@ -221,8 +240,57 @@
         for i in range(5):
             tasks[f"{R}{i}"] = lambda i=i: first(i)
 
+        def fbuf(b, d, s):
+            return rows_of(b * 6 + "pm".index(d) * 3 + "abc".index(s))
+
+        def ywhole(b, d, s):
+            near = 1 if d == "p" else 3
+            h = 0 if d == "p" else 1
+            if s == "b":
+                h = 1 - h
+            v = src[h, rows_of(b * 4 + (y + (2 if s == "a" else near)) % 4), :]
+            if s == "c":
+                got(f"{R}y{b}{d}a")
+                v = v + y_recv[fbuf(b, d, "a"), :].astype(F32)
+            mine = fbuf(b, d, s)
+            y_send[mine, :] = v.astype(BF)
+            send(f"{R}y{b}{d}{s}", y_send.at[mine], y_recv.at[mine], yside[d])
+
+        def xwhole(b, h):
+            p, m = ("c", "b") if h == 0 else ("b", "c")
+            got(f"{R}y{b}p{p}", f"{R}y{b}m{m}")
+            rows = rows_of(b * 2 + h)
+            t = (src[h, rows_of(b * 4 + y), :] + y_recv[fbuf(b, "p", p), :].astype(F32)
+                 + y_recv[fbuf(b, "m", m), :].astype(F32))
+            hid[rows, :] = t
+            h_send[rows, :] = t.astype(BF)
+            send(f"{R}x{b}{h}", h_send.at[rows], h_recv.at[rows], across)
+
+        def ewhole(b, h):
+            got(f"{R}x{b}{h}")
+            rows = rows_of(b * 2 + h)
+            mine = lhs2.at[h, rows_of(b * 4 + y)]
+            mine[...] = finish(hid[rows, :] + h_recv[rows, :].astype(F32), rows).astype(BF)
+            for d in "pm":
+                send(f"{R}o{b}{h}{d}", mine, mine, yside[d])
+
+        def fwhole(b, d):
+            h, yy = (0, (y + 3) % 4) if d == "p" else (1, (y + 1) % 4)
+            got(f"{R}o{b}{h}{d}")
+            p = lhs2.at[h, rows_of(b * 4 + yy)]
+            send(f"{R}f{b}{d}", p, p, yside[d])
+
+        for b in (0, 1) if n == 0 else ():
+            for d in "pm":
+                for s in "abc":
+                    tasks[f"{R}y{b}{d}{s}"] = lambda b=b, d=d, s=s: ywhole(b, d, s)
+                tasks[f"{R}f{b}{d}"] = lambda b=b, d=d: fwhole(b, d)
+            for h in (0, 1):
+                tasks[f"{R}x{b}{h}"] = lambda b=b, h=h: xwhole(b, h)
+                tasks[f"{R}e{b}{h}"] = lambda b=b, h=h: ewhole(b, h)
+
         def xbuf(p):
-            return rows_of(n * 8 + p) if isinstance(p, int) else pl.ds(pl.multiple_of((n * 8 + p) * TOK, TOK), TOK)
+            return rows_of(p)
 
         def xstep(p):
             x_send[xbuf(p), :] = src[1 - xh, rows_of(p), :].astype(BF)
@@ -231,11 +299,11 @@
         def paired(p, r):
             start, many = SUB[r]
             rows = pl.ds(pl.multiple_of(p * TOK + start, 16), many)
-            far = pl.ds(pl.multiple_of((n * 8 + p) * TOK + start, 16), many)
+            far = pl.ds(pl.multiple_of(p * TOK + start, 16), many)
             return src[xh, rows, :] + x_recv[far, :].astype(F32)
 
         def ybuf(b, d, s, r):
-            return pl.ds(((n * 2 + b) * 6 + "pm".index(d) * 3 + "abc".index(s)) * SUB[0][1], SUB[r][1])
+            return pl.ds(12 * TOK + (b * 6 + "pm".index(d) * 3 + "abc".index(s)) * SUB[0][1], SUB[r][1])
 
         def ystep(b, d, s):
             got(*(f"{R}x{b * 4 + i}" for i in range(4)))
@@ -261,7 +329,7 @@
                 v = (paired(b * 4 + y, r) + y_recv[ybuf(b, "p", p, r), :].astype(F32)
                      + y_recv[ybuf(b, "m", m, r), :].astype(F32))
                 start, many = SUB[r]
-                v = finish(v, pl.ds(b * TOK + start, many)).astype(BF)
+                v = finish(v, pl.ds(pl.multiple_of((b * 2 + xh) * TOK + start, 16), many)).astype(BF)
                 lhs2[xh, pl.ds(pl.multiple_of((b * 4 + y) * TOK + start, 16), many), :] = v
             mine = piece(b, y, xh)
             for d in "pm":
@@ -283,9 +351,9 @@
                 p = piece(b, (y + 1) % 4, 1 - xh)
             send(f"{R}f{b}{d}", p, p, yside[d])
 
-        for p in range(8):
+        for p in range(8 if n == 1 else 0):
             tasks[f"{R}x{p}"] = lambda p=p: xstep(p)
-        for b in (0, 1):
+        for b in (0, 1) if n == 1 else ():
             for d in "pm":
                 for s in "abc":
                     tasks[f"{R}y{b}{d}{s}"] = lambda b=b, d=d, s=s: ystep(b, d, s)
@@ -295,7 +363,8 @@
 
         def second(i):
             for b in {0: (0,), 1: (0,), 2: (0, 1), 3: (1,), 4: (1,)}[i]:
-                got(*(f"{R}{q}{b}{d}" for q in "onf" for d in "pm"))
+                got(*(f"{R}{q}{b}{d}" for q in "fon" for d in "pm" if f"{R}{q}{b}{d}" in msg),
+                    *(f"{R}o{b}{h}{d}" for h in (0, 1) for d in "pm" if f"{R}o{b}{h}{d}" in msg))
             got("down", "W2")
             product(lhs2, rhs2, src, i)
 
@@ -315,51 +384,78 @@
                 got(f"{N}r{d}{i - 2}")
                 v = v + z_recv[zbuf(d, i - 2), :].astype(F32)
             z_send[zbuf(d, i), :] = v.astype(BF)
-            send(f"{N}r{d}{i}", z_send.at[zbuf(d, i)], z_recv.at[zbuf(d, i)], zside[d])
+            if i < 5:
+                send(f"{N}r{d}{i}", z_send.at[zbuf(d, i)], z_recv.at[zbuf(d, i)], zside[d])
+                return
+            there = rows_of(n * 4 + "pm".index(d) * 2 + i - 5)
+            straight = remote(z_send.at[zbuf(d, i)], z_recv.at[zbuf(d, i)], zside[d])
+            aslant = remote(z_send.at[zbuf(d, i)], s_recv.at[there], slant[d])
+            pl.when(xl == k)(straight.start)
+            pl.when(xl != k)(aslant.start)
+            ends.append(unless(xl == k, straight.wait_send))
+            ends.append(unless(xl != k, aslant.wait_send))
+            msg[f"{N}r{d}{i}"] = straight.wait_recv
+            msg[f"{N}s{d}{i}"] = aslant.wait_recv
 
         for d in "pm":
             for i in range(7):
                 tasks[f"{N}r{d}{i}"] = lambda d=d, i=i: zstep(d, i)
 
-        def tstep(h):
-            p, m = (6, 5) if h == 0 else (5, 6)
-            got(f"{N}rp{p}", f"{N}rm{m}")
-            mine = rows_of(n * 2 + h)
-            f_send[mine, :] = (src[h, rows_of(0), :] + z_recv[zbuf("p", p), :].astype(F32)
-                               + z_recv[zbuf("m", m), :].astype(F32))
-            if f"{N}far" not in msg:
-                msg[f"{N}far"], msg[f"{N}near"] = sem(), sem()
-            i, j = msg[f"{N}far"], msg[f"{N}near"]
-            far = pltpu.make_async_remote_copy(
-                src_ref=f_send.at[mine], dst_ref=f_recv.at[rows_of(2 * n)],
-                send_sem=ssem.at[i if h == 0 else sem()], recv_sem=rsem.at[i],
-                device_id=other[h], device_id_type=MESH)
-            near = pltpu.make_async_remote_copy(
-                src_ref=f_send.at[mine], dst_ref=f_recv.at[rows_of(2 * n + 1)],
-                send_sem=ssem.at[j], recv_sem=rsem.at[j], device_id=mate, device_id_type=MESH)
-            pl.when(xl != k)(far.start)
-            give = jnp.logical_and(xl == k, k != h)
-            pl.when(give)(near.start)
-            ends.append(unless(xl != k, far.wait_send))
-            ends.append(unless(give, near.wait_send))
-            msg[f"{N}o"] = (far.wait_recv, near.wait_recv)
-
-        def ostep():
-            far, near = msg[f"{N}o"]
-            far()
-            mine = rows_of(n)
+        def wstep():
+            cps = []
+            for h in (0, 1):
+                mine = rows_of(n * 2 + h)
+                cps.append(remote(w_send.at[mine], w_recv.at[mine], (r, other_c)))
 
             @pl.when(xl != k)
             def _():
-                near()
-                small[mine, :] = (f_recv[rows_of(2 * n), :] + f_recv[rows_of(2 * n + 1), :]).astype(BF)
+                for h in (0, 1):
+                    w_send[rows_of(n * 2 + h), :] = src[h, rows_of(0), :].astype(BF)
+                for cp in cps:
+                    cp.start()
+
+            for h, cp in enumerate(cps):
+                ends.append(unless(xl != k, cp.wait_send))
+                msg[f"{N}w{h}"] = cp.wait_recv
+
+        def tstep(h):
+            mine = rows_of(n * 2 + h)
+            cp = remote(f_send.at[mine], f_recv.at[rows_of(n)], mate)
 
             @pl.when(xl == k)
             def _():
-                small[mine, :] = (f_recv[rows_of(2 * n), :] + f_send[rows_of(n * 2 + k), :]).astype(BF)
+                v = src[h, rows_of(0), :]
+                msg[f"{N}w{h}"]()
+                v = v + w_recv[mine, :].astype(F32)
+                for d in "pm":
+                    i = 6 if (h == 0) == (d == "p") else 5
+                    msg[f"{N}r{d}{i}"]()
+                    msg[f"{N}s{d}{i}"]()
+                    there = rows_of(n * 4 + "pm".index(d) * 2 + i - 5)
+                    v = v + z_recv[zbuf(d, i), :].astype(F32) + s_recv[there, :].astype(F32)
+                f_send[mine, :] = v
+                pl.when(k != h)(cp.start)
+
+            give = jnp.logical_and(xl == k, k != h)
+            ends.append(unless(give, cp.wait_send))
+            msg[f"{N}t{h}"] = unless(jnp.logical_and(xl != k, k == h), cp.wait_recv)
+
+        def ostep():
+            mine = rows_of(n)
+            msg[f"{N}t0"]()
+            msg[f"{N}t1"]()
+
+            @pl.when(xl != k)
+            def _():
+                small[mine, :] = f_recv[mine, :].astype(BF)
+
+            @pl.when(xl == k)
+            def _():
+                small[mine, :] = f_send[rows_of(n * 2 + k), :].astype(BF)
 
             ends.append(lcopy(small.at[mine], (mixed_out, igrad_out)[n]))
 
+        tasks[f"{N}w"] = wstep
         tasks[f"{N}t0"], tasks[f"{N}t1"], tasks[f"{N}o"] = lambda: tstep(0), lambda: tstep(1), ostep
 
     def forward(v, rows):
@@ -463,15 +559,18 @@
             vm((2, 2 * ROWS, HALF), BF), vm((2, 2 * ROWS, HALF), BF),
             vm((ROWS, HALF), BF), vm((ROWS, HALF), BF),
             vm((2, 2, ROWS, HALF), F32),
-            vm((2 * TOK, HALF), F32),
-            vm((16 * TOK, HALF), BF), vm((16 * TOK, HALF), BF),
-            vm((24 * 48, HALF), BF), vm((24 * 48, HALF), BF),
+            vm((4 * TOK, HALF), F32),
+            vm((4 * TOK, HALF), BF), vm((4 * TOK, HALF), BF),
+            vm((8 * TOK, HALF), BF), vm((8 * TOK, HALF), BF),
+            vm((12 * 128, HALF), BF), vm((12 * 128, HALF), BF),
             vm((28 * TOK, HALF), BF), vm((28 * TOK, HALF), BF),
-            vm((4 * TOK, HALF), F32), vm((4 * TOK, HALF), F32),
+            vm((8 * TOK, HALF), BF),
+            vm((4 * TOK, HALF), BF), vm((4 * TOK, HALF), BF),
+            vm((4 * TOK, HALF), F32), vm((2 * TOK, HALF), F32),
             vm((HALF, WIDE), BF), vm((WIDE, HALF), BF),
             vm((2 * TOK, HALF), BF),
-            pltpu.SemaphoreType.DMA((160,)),
-            pltpu.SemaphoreType.DMA((160,)),
+            pltpu.SemaphoreType.DMA((192,)),
+            pltpu.SemaphoreType.DMA((192,)),
             pltpu.SemaphoreType.DMA((16,)),
         ],
         compiler_params=pltpu.CompilerParams(

time: 116 us -> 112 us (0.966)
  Pallas kernels: 114 us -> 111 us
    pallas_call x1, Pallas kernels: 111 us -> 108 us  [local(): pl.pallas_call(kernel, name='ffn', out_shape=(jax.ShapeDtypeStruct((TOK,...]
where the time goes in v3:
time: 112 us
  Pallas kernels  111 us (99%)
    pallas_call x1, Pallas kernels, local(): pl.pallas_call(kernel, name='ffn', out_shape=(jax.ShapeDtypeStruct((TOK,...  108 us
    pallas_call x1, Pallas kernels, local(): pl.pallas_call(hand_on, name='hand_on', out_shape=[jax.ShapeDtypeStruct(x...  2.93 us

profile of v3, /device:TPU:8, one launch (start us, length us, event | category | flops | bytes accessed | tf_op | source)
XLA Modules:
  0.0 111.9 jit_solution(2585071443391791612)
XLA Ops:
  0.6 108.2 %ffn.1 = (bf16[80,640]{1,0:T(8,128)(2,1)}, bf16[80,640]{1,0:T(8,128)(2,1)}, bf16[640,1280]{1,0:T(8,128)(2,1)}, bf16[1280,640]{1,0:T(8,128)(2,1)}) custom-call(bf16[80,640]{1,0:T(8,128)(2,1)} %tok_in.1, bf16[640,1280]{1,0:T(8,128)(2,1)} %up_in.1, bf16[1280,640]{1,0:T(8,128)(2,1)} %down_in.1, bf16[80,640]{1,0:T(8,128)(2,1)} %grad_in.1), custom_call_target="tpu_custom_call" | custom-call | flops 12600000512 | bytes 10000000 | tf_op jit(solution)/shard_map/ffn/pallas_call | solution.py:544
  108.8 2.9 %hand_on.1 = (bf16[80,640]{1,0:T(8,128)(2,1)}, bf16[80,640]{1,0:T(8,128)(2,1)}, bf16[640,1280]{1,0:T(8,128)(2,1)}, bf16[1280,640]{1,0:T(8,128)(2,1)}) custom-call(bf16[80,640]{1,0:T(8,128)(2,1)} %get-tuple-element.8.a, bf16[80,640]{1,0:T(8,128)(2,1)} %get-tuple-element.9.b, bf16[640,1280]{1,0:T(8,128)(2,1)} %get-tuple-element.10.c, ...), custom_call_target="tpu_custom_call" | custom-call | bytes 8000000 | tf_op jit(solution)/shard_map/hand_on/pallas_call | solution.py:581

commit v4 on v3

--- a/solution.py
+++ b/solution.py
@@ -22,18 +22,20 @@
 C1 = 0.044715
 
 ORDER = (
-    "Gs", "W1s", "W2s", "Tzp2", "Tzm2", "P1", "Tzm3", "Gzm2", "Tzp3", "P0", "D", "Gzp3",
-    "Tzp4", "Tzm4", "Gzm3", "Gzp2", "Q1", "Tzp5", "P2", "Qx2", "Py0pa", "Py0ma", "Qx1", "Tzm5",
-    "Py0pb", "Tzp6", "Tzm6", "Q0", "Py0mb", "Qx0", "Gzm4", "Gzp4", "Gzp5", "Q2", "Py0pc", "Py0mc",
-    "Gzm5", "Qx4", "P3", "Qx3", "P4", "Py1pa", "Gzm6", "Py1ma", "Gzp6", "Py1pb", "Px01", "Py1mb",
-    "Q3", "Qx6", "Py1pc", "Qx5", "Py1mc", "Qy0pa", "Q4", "Qy0ma", "Qx7", "Pe01", "Px10", "Qy0mb",
-    "Gm", "Qy0mc", "Px11", "Qy0pc", "Qy0pb", "Qy1mb", "Qy1pb", "Qy1ma", "Px00", "Qy1pa", "Pe10", "Pe11",
-    "Qy1pc", "Qy1mc", "U", "Tm", "Pf1p", "Pf1m", "Pf0m", "Pe00", "Qe1", "M4", "Mrp0", "Mrm0",
-    "Pf0p", "M3", "Mrp1", "Mrm1", "Qn1", "Qe0", "Qf1p", "Mrp2", "Mrm2", "M2", "Mrp3", "Mrm3",
-    "Qf1m", "Am", "Qn0", "Mrp4", "Mrm4", "M1", "Mrp5", "Mrm5", "I4", "Irp0", "Irm0", "Qf0p",
-    "I3", "Qf0m", "Irm1", "Irp1", "M0", "DG3", "Irp2", "Irm2", "Mrp6", "I2", "Irm3", "I1",
-    "Mw", "Irp4", "Irm4", "I0", "Irp3", "Mrm6", "DG1", "Hm", "Iw", "Irm5", "Irp6", "DG0",
-    "Irm6", "Irp5", "Mt0", "Mt1", "DG2", "UG0", "Mo", "It0", "It1", "UG1", "Io",
+    "W2s", "Gs", "W1s", "D", "Tzm2", "Tzp2", "Tzp3", "Tzm3", "P0", "Gzm2", "Gzp2", "Q1",
+    "Tzp4", "Tzm4", "P1", "Gzm3", "Qx2", "Gzp3", "P2", "Py0ma", "Tzm5", "Py0pa", "Py0mb", "Tzp5",
+    "Qx1", "Q0", "Tzm6", "Tzp6", "Qx0", "Gzp4", "Py0pb", "Q2", "Py0mc", "Qx3", "Gzm4", "Py0pc",
+    "Qx4", "Gzm5", "Gzp5", "P3", "P4", "Py1ma", "Py1pa", "Px01", "Gzm6", "Py1mb", "Gzp6", "Px00",
+    "Qy0ma", "Qy0pa", "Py1pb", "Q3", "Qx5", "Py1mc", "Qx6", "Py1pc", "Pe01", "Q4", "Qx7", "Qy0mb",
+    "Pe00", "Qy0pb", "Qy0pc", "Px10", "Px11", "Pf0m", "U", "Qy1ma", "Qy1pa", "Qy1mb", "Qy1pb", "Pe10",
+    "Tm", "Qy1mc", "Qy1pc", "Pf0p", "Pe11", "Pf1p", "Qy0mc", "Qe1", "Pf1m", "M1", "Gm", "Mu2",
+    "Mu1", "M0", "Mw", "Qn1", "Qe0", "M4", "Mrp0", "Mu7", "M3", "Mrm1", "Qf1p", "Qf1m",
+    "Mu5", "Mu6", "M2", "Qn0", "Am", "Mrp2", "Mu4", "Qf0p", "Mu3", "Mrm0", "Mrp1", "Mrm3",
+    "I4", "Irp0", "Iu7", "I3", "Qf0m", "Mrm2", "Mrp4", "Iu5", "Iu6", "Irm1", "Mu0", "Mrp3",
+    "Irm0", "DG3", "Irp2", "Mrm5", "Mrm4", "Irp1", "I2", "Iu3", "Mrp5", "I0", "Irm2", "Iu4",
+    "Irp4", "Irm3", "I1", "Hm", "Irp3", "Iu1", "Mrm6", "Iu2", "Mrp6", "Irm4", "Iu0", "DG0",
+    "Irp6", "Irm5", "DG1", "Irp5", "Iw", "DG2", "Irm6", "UG0", "Mt1", "Mt0", "It0", "It1",
+    "UG1", "Mo", "Io",
 )
 
 
@@ -62,7 +64,7 @@
     tok_in, up_in, down_in, grad_in,
     mixed_out, igrad_out, upg_out, downg_out,
     up, down, up_t, down_t, tok, grad, act, hgrad, tok_o, grad_o,
-    part, hid, h_send, h_recv, x_send, x_recv, y_send, y_recv, z_send, z_recv, s_recv, w_send, w_recv, f_send, f_recv,
+    part, hid, h_send, h_recv, x_send, x_recv, y_send, y_recv, z_send, z_recv, u_send, u_recv, s_recv, w_send, w_recv, f_send, f_recv,
     upg, downg, small,
     ssem, rsem, lsem,
 ):
@@ -374,49 +376,76 @@
         def zbuf(d, i):
             return rows_of(n * 14 + "pm".index(d) * 7 + i)
 
+        def ubuf(p):
+            return rows_of(n * 8 + p)
+
+        def ustep(p):
+            cp = remote(u_send.at[ubuf(p)], u_recv.at[ubuf(p)], (r, other_c))
+
+            @pl.when(xl != k)
+            def _():
+                u_send[ubuf(p), :] = src[1, rows_of(p), :].astype(BF)
+                cp.start()
+
+            ends.append(unless(xl != k, cp.wait_send))
+            msg[f"{N}u{p}"] = cp.wait_recv
+
+        for p in range(8):
+            tasks[f"{N}u{p}"] = lambda p=p: ustep(p)
+
         def zstep(d, i):
             first = 0 if d == "p" else 1
             h = first if i % 2 == 0 else 1 - first
             o = 4 - (i + 1) // 2
             place = PLACE[o if d == "p" or o == 4 else -o]
-            v = src[h, rows_of(place), :]
+            mine = zbuf(d, i)
+            straight = remote(z_send.at[mine], z_recv.at[mine], zside[d])
+            msg[f"{N}r{d}{i}"] = straight.wait_recv
+            if h == 1:
+                @pl.when(xl == k)
+                def _():
+                    msg[f"{N}u{place}"]()
+                    v = src[1, rows_of(place), :] + u_recv[ubuf(place), :].astype(F32)
+                    if i >= 2:
+                        msg[f"{N}r{d}{i - 2}"]()
+                        v = v + z_recv[zbuf(d, i - 2), :].astype(F32)
+                    z_send[mine, :] = v.astype(BF)
+                    straight.start()
+
+                ends.append(unless(xl == k, straight.wait_send))
+                return
+            v = src[0, rows_of(place), :]
             if i >= 2:
-                got(f"{N}r{d}{i - 2}")
+                msg[f"{N}r{d}{i - 2}"]()
                 v = v + z_recv[zbuf(d, i - 2), :].astype(F32)
-            z_send[zbuf(d, i), :] = v.astype(BF)
+            z_send[mine, :] = v.astype(BF)
             if i < 5:
-                send(f"{N}r{d}{i}", z_send.at[zbuf(d, i)], z_recv.at[zbuf(d, i)], zside[d])
+                straight.start()
+                ends.append(straight.wait_send)
                 return
-            there = rows_of(n * 4 + "pm".index(d) * 2 + i - 5)
-            straight = remote(z_send.at[zbuf(d, i)], z_recv.at[zbuf(d, i)], zside[d])
-            aslant = remote(z_send.at[zbuf(d, i)], s_recv.at[there], slant[d])
+            there = rows_of(n * 2 + "pm".index(d))
+            aslant = remote(z_send.at[mine], s_recv.at[there], slant[d])
             pl.when(xl == k)(straight.start)
             pl.when(xl != k)(aslant.start)
             ends.append(unless(xl == k, straight.wait_send))
             ends.append(unless(xl != k, aslant.wait_send))
-            msg[f"{N}r{d}{i}"] = straight.wait_recv
-            msg[f"{N}s{d}{i}"] = aslant.wait_recv
+            msg[f"{N}s{d}"] = aslant.wait_recv
 
         for d in "pm":
             for i in range(7):
                 tasks[f"{N}r{d}{i}"] = lambda d=d, i=i: zstep(d, i)
 
         def wstep():
-            cps = []
-            for h in (0, 1):
-                mine = rows_of(n * 2 + h)
-                cps.append(remote(w_send.at[mine], w_recv.at[mine], (r, other_c)))
+            mine = rows_of(n)
+            cp = remote(w_send.at[mine], w_recv.at[mine], (r, other_c))
 
             @pl.when(xl != k)
             def _():
-                for h in (0, 1):
-                    w_send[rows_of(n * 2 + h), :] = src[h, rows_of(0), :].astype(BF)
-                for cp in cps:
-                    cp.start()
-
-            for h, cp in enumerate(cps):
-                ends.append(unless(xl != k, cp.wait_send))
-                msg[f"{N}w{h}"] = cp.wait_recv
+                w_send[mine, :] = src[0, rows_of(0), :].astype(BF)
+                cp.start()
+
+            ends.append(unless(xl != k, cp.wait_send))
+            msg[f"{N}w"] = cp.wait_recv
 
         def tstep(h):
             mine = rows_of(n * 2 + h)
@@ -425,14 +454,19 @@
             @pl.when(xl == k)
             def _():
                 v = src[h, rows_of(0), :]
-                msg[f"{N}w{h}"]()
-                v = v + w_recv[mine, :].astype(F32)
+                if h == 0:
+                    msg[f"{N}w"]()
+                    v = v + w_recv[rows_of(n), :].astype(F32)
+                else:
+                    msg[f"{N}u0"]()
+                    v = v + u_recv[ubuf(0), :].astype(F32)
                 for d in "pm":
                     i = 6 if (h == 0) == (d == "p") else 5
                     msg[f"{N}r{d}{i}"]()
-                    msg[f"{N}s{d}{i}"]()
-                    there = rows_of(n * 4 + "pm".index(d) * 2 + i - 5)
-                    v = v + z_recv[zbuf(d, i), :].astype(F32) + s_recv[there, :].astype(F32)
+                    v = v + z_recv[zbuf(d, i), :].astype(F32)
+                    if h == 0:
+                        msg[f"{N}s{d}"]()
+                        v = v + s_recv[rows_of(n * 2 + "pm".index(d)), :].astype(F32)
                 f_send[mine, :] = v
                 pl.when(k != h)(cp.start)
 
@@ -564,8 +598,9 @@
             vm((8 * TOK, HALF), BF), vm((8 * TOK, HALF), BF),
             vm((12 * 128, HALF), BF), vm((12 * 128, HALF), BF),
             vm((28 * TOK, HALF), BF), vm((28 * TOK, HALF), BF),
-            vm((8 * TOK, HALF), BF),
-            vm((4 * TOK, HALF), BF), vm((4 * TOK, HALF), BF),
+            vm((16 * TOK, HALF), BF), vm((16 * TOK, HALF), BF),
+            vm((4 * TOK, HALF), BF),
+            vm((2 * TOK, HALF), BF), vm((2 * TOK, HALF), BF),
             vm((4 * TOK, HALF), F32), vm((2 * TOK, HALF), F32),
             vm((HALF, WIDE), BF), vm((WIDE, HALF), BF),
             vm((2 * TOK, HALF), BF),

time: 112 us -> 109 us (0.973)
  Pallas kernels: 111 us -> 107 us
    pallas_call x1, Pallas kernels: 108 us -> 104 us  [local(): pl.pallas_call(kernel, name='ffn', out_shape=(jax.ShapeDtypeStruct((TOK,...]
where the time goes in v4:
time: 109 us; the launch traced here: 108 us
  Pallas kernels  107 us (98%)
    pallas_call x1, Pallas kernels, local(): pl.pallas_call(kernel, name='ffn', out_shape=(jax.ShapeDtypeStruct((TOK,...  104 us
    pallas_call x1, Pallas kernels, local(): pl.pallas_call(hand_on, name='hand_on', out_shape=[jax.ShapeDtypeStruct(x...  2.93 us

profile of v4, /device:TPU:8, one launch (start us, length us, event | category | flops | bytes accessed | tf_op | source)
XLA Modules:
  0.0 108.2 jit_solution(5196453121382559325)
XLA Ops:
  0.6 104.5 %ffn.1 = (bf16[80,640]{1,0:T(8,128)(2,1)}, bf16[80,640]{1,0:T(8,128)(2,1)}, bf16[640,1280]{1,0:T(8,128)(2,1)}, bf16[1280,640]{1,0:T(8,128)(2,1)}) custom-call(bf16[80,640]{1,0:T(8,128)(2,1)} %tok_in.1, bf16[640,1280]{1,0:T(8,128)(2,1)} %up_in.1, bf16[1280,640]{1,0:T(8,128)(2,1)} %down_in.1, bf16[80,640]{1,0:T(8,128)(2,1)} %grad_in.1), custom_call_target="tpu_custom_call" | custom-call | flops 12600000512 | bytes 10000000 | tf_op jit(solution)/shard_map/ffn/pallas_call | solution.py:578
  105.1 2.9 %hand_on.1 = (bf16[80,640]{1,0:T(8,128)(2,1)}, bf16[80,640]{1,0:T(8,128)(2,1)}, bf16[640,1280]{1,0:T(8,128)(2,1)}, bf16[1280,640]{1,0:T(8,128)(2,1)}) custom-call(bf16[80,640]{1,0:T(8,128)(2,1)} %get-tuple-element.8.a, bf16[80,640]{1,0:T(8,128)(2,1)} %get-tuple-element.9.b, bf16[640,1280]{1,0:T(8,128)(2,1)} %get-tuple-element.10.c, ...), custom_call_target="tpu_custom_call" | custom-call | bytes 8000000 | tf_op jit(solution)/shard_map/hand_on/pallas_call | solution.py:616

commit v5 on v4

--- a/solution.py
+++ b/solution.py
@@ -64,7 +64,7 @@
     tok_in, up_in, down_in, grad_in,
     mixed_out, igrad_out, upg_out, downg_out,
     up, down, up_t, down_t, tok, grad, act, hgrad, tok_o, grad_o,
-    part, hid, h_send, h_recv, x_send, x_recv, y_send, y_recv, z_send, z_recv, u_send, u_recv, s_recv, w_send, w_recv, f_send, f_recv,
+    part, hid, h_send, h_recv, x_send, x_recv, y_send, y_recv, z_send, z_recv, u_send, u_recv, s_recv, w_send, w_recv,
     upg, downg, small,
     ssem, rsem, lsem,
 ):
@@ -449,7 +449,10 @@
 
         def tstep(h):
             mine = rows_of(n * 2 + h)
-            cp = remote(f_send.at[mine], f_recv.at[rows_of(n)], mate)
+            out = (mixed_out, igrad_out)[n]
+            cp = remote(small.at[mine], out, mate)
+            stay = pltpu.make_async_copy(small.at[mine], out, lsem.at[count[1]])
+            count[1] += 1
 
             @pl.when(xl == k)
             def _():
@@ -467,27 +470,18 @@
                     if h == 0:
                         msg[f"{N}s{d}"]()
                         v = v + s_recv[rows_of(n * 2 + "pm".index(d)), :].astype(F32)
-                f_send[mine, :] = v
+                small[mine, :] = v.astype(BF)
                 pl.when(k != h)(cp.start)
+                pl.when(k == h)(stay.start)
 
             give = jnp.logical_and(xl == k, k != h)
             ends.append(unless(give, cp.wait_send))
+            ends.append(unless(jnp.logical_and(xl == k, k == h), stay.wait))
             msg[f"{N}t{h}"] = unless(jnp.logical_and(xl != k, k == h), cp.wait_recv)
 
         def ostep():
-            mine = rows_of(n)
             msg[f"{N}t0"]()
             msg[f"{N}t1"]()
-
-            @pl.when(xl != k)
-            def _():
-                small[mine, :] = f_recv[mine, :].astype(BF)
-
-            @pl.when(xl == k)
-            def _():
-                small[mine, :] = f_send[rows_of(n * 2 + k), :].astype(BF)
-
-            ends.append(lcopy(small.at[mine], (mixed_out, igrad_out)[n]))
 
         tasks[f"{N}w"] = wstep
         tasks[f"{N}t0"], tasks[f"{N}t1"], tasks[f"{N}o"] = lambda: tstep(0), lambda: tstep(1), ostep
@@ -601,9 +595,8 @@
             vm((16 * TOK, HALF), BF), vm((16 * TOK, HALF), BF),
             vm((4 * TOK, HALF), BF),
             vm((2 * TOK, HALF), BF), vm((2 * TOK, HALF), BF),
-            vm((4 * TOK, HALF), F32), vm((2 * TOK, HALF), F32),
             vm((HALF, WIDE), BF), vm((WIDE, HALF), BF),
-            vm((2 * TOK, HALF), BF),
+            vm((4 * TOK, HALF), BF),
             pltpu.SemaphoreType.DMA((192,)),
             pltpu.SemaphoreType.DMA((192,)),
             pltpu.SemaphoreType.DMA((16,)),

time: 109 us -> 108 us (level)
  no operation moved by 1% of the time
where the time goes in v5:
time: 108 us
  Pallas kernels  107 us (99%)
    pallas_call x1, Pallas kernels, local(): pl.pallas_call(kernel, name='ffn', out_shape=(jax.ShapeDtypeStruct((TOK,...  104 us
    pallas_call x1, Pallas kernels, local(): pl.pallas_call(hand_on, name='hand_on', out_shape=[jax.ShapeDtypeStruct(x...  2.93 us

profile of v5, /device:TPU:8, one launch (start us, length us, event | category | flops | bytes accessed | tf_op | source)
XLA Modules:
  0.0 107.8 jit_solution(15741425131239186658)
XLA Ops:
  0.6 104.0 %ffn.1 = (bf16[80,640]{1,0:T(8,128)(2,1)}, bf16[80,640]{1,0:T(8,128)(2,1)}, bf16[640,1280]{1,0:T(8,128)(2,1)}, bf16[1280,640]{1,0:T(8,128)(2,1)}) custom-call(bf16[80,640]{1,0:T(8,128)(2,1)} %tok_in.1, bf16[640,1280]{1,0:T(8,128)(2,1)} %up_in.1, bf16[1280,640]{1,0:T(8,128)(2,1)} %down_in.1, bf16[80,640]{1,0:T(8,128)(2,1)} %grad_in.1), custom_call_target="tpu_custom_call" | custom-call | flops 12600000512 | bytes 10000000 | tf_op jit(solution)/shard_map/ffn/pallas_call | solution.py:572
  104.7 2.9 %hand_on.1 = (bf16[80,640]{1,0:T(8,128)(2,1)}, bf16[80,640]{1,0:T(8,128)(2,1)}, bf16[640,1280]{1,0:T(8,128)(2,1)}, bf16[1280,640]{1,0:T(8,128)(2,1)}) custom-call(bf16[80,640]{1,0:T(8,128)(2,1)} %get-tuple-element.8.a, bf16[80,640]{1,0:T(8,128)(2,1)} %get-tuple-element.9.b, bf16[640,1280]{1,0:T(8,128)(2,1)} %get-tuple-element.10.c, ...), custom_call_target="tpu_custom_call" | custom-call | bytes 8000000 | tf_op jit(solution)/shard_map/hand_on/pallas_call | solution.py:609
